TPU v7x, 512 devices: a whole 4x8x8 slice. The times are simulated.
512 devices in a mesh: tok: 64 (over y, x, core), hid: 8 (over z).
Axes of the slice: x: 4, y: 8, z: 8, core: 2. Of those that a mesh axis runs over, the one named last changes fastest.
Arguments:
- acts: bfloat16 [32768, 14336], P('tok', 'hid'), may hold values from -6 to 6
- dictionary: float32 [14336, 256], P('hid'), may hold values from -0.046875 to 0.046875
- codes: float32 [32768, 256], P('tok'), may hold values from 0.02 to 1, as said below
Outputs:
- codes_out: float32 [32768, 256], P('tok')
- dict_out: float32 [14336, 256], P('hid')
Inputs may be any that keep to these rules, and one draw needn't show every extreme that they name: `codes`: every starting code is positive.
All inputs are finite; a program needn't handle non-finite values.
Results may differ from a plain program's by a relative error of at most 0.0043.
Values sent between devices are 32-bit elements; how exact they have to be, the bound alone decides.
A program may use at most 64 MiB of HBM per device.

v0:
```python
import jax
import jax.numpy as jnp
from jax import lax
from jax.sharding import PartitionSpec as P

floor_value = 0.05


def refine(codes, proj, gram):
    gram_pos = jnp.maximum(gram, 0.0)
    gram_neg = jnp.maximum(-gram, 0.0)
    numer = jnp.maximum(proj, 0.0) + jnp.dot(codes, gram_neg, precision=lax.Precision.HIGHEST)
    denom = jnp.maximum(
        jnp.maximum(-proj, 0.0) + jnp.dot(codes, gram_pos, precision=lax.Precision.HIGHEST),
        floor_value,
    )
    return codes * jnp.sqrt(numer / denom)


def solve_rows(cross, gram):
    lower = jnp.linalg.cholesky(gram)
    return jax.scipy.linalg.cho_solve((lower, True), cross.T).T


def self_gram(matrix):
    return jnp.dot(matrix.T, matrix, precision=lax.Precision.HIGHEST)


def per_device(acts, dictionary, codes):
    proj_part = jnp.dot(acts, dictionary.astype(jnp.bfloat16), preferred_element_type=jnp.float32)
    proj, gram_dict = lax.psum((proj_part, self_gram(dictionary)), "hid")
    codes_mid = refine(codes, proj, gram_dict)
    codes_low = codes_mid.astype(jnp.bfloat16)
    cross_part = lax.dot_general(
        acts, codes_low, (((0,), (0,)), ((), ())), preferred_element_type=jnp.float32
    )
    gram_part = jnp.dot(codes_low.T, codes_low, preferred_element_type=jnp.float32)
    cross, gram_codes = lax.psum((cross_part, gram_part), "tok")
    dict_out = solve_rows(cross, gram_codes)
    proj_next = jnp.dot(acts, dict_out.astype(jnp.bfloat16), preferred_element_type=jnp.float32)
    proj_two, gram_new = lax.psum((proj_next, self_gram(dict_out)), "hid")
    codes_out = refine(codes_mid, proj_two, gram_new)
    return (codes_out, dict_out)


def solution(mesh):
    return jax.shard_map(
        per_device,
        mesh=mesh,
        in_specs=(P("tok", "hid"), P("hid", None), P("tok", None)),
        out_specs=(P("tok", None), P("hid", None)),
        check_vma=False,
    )
```

profile of v0, /device:TPU:1, one launch (start us, length us, event | category | flops | bytes accessed | tf_op | source)
XLA Modules:
  0.0 464.4 jit_solution(9830523844437436010)
XLA Ops:
  7.2 6.0 %fusion.47 = f32[256,256]{1,0:T(8,128)} fusion(f32[1792,256]{1,0:T(8,128)} %param.4), kind=kOutput, calls=%fused_computation.72 | convolution fusion | flops 1409286144 | bytes 2097152 | tf_op jit(solution)/shard_map/dot_general | solution.py:26
  13.2 1.5 fusion.15
  14.7 82.3 %all-reduce.12.cloned.1.call-done = (f32[512,256]{1,0:T(8,128)}, f32[256,256]{1,0:T(8,128)}) async-done(((f32[512,256]{1,0:T(8,128)}, f32[256,256]{1,0:T(8,128)}), (f32[512,256]{1,0:T(8,128)}, f32[256,256]{1,0:T(8,128)})) %all-reduce.12.cloned.1.call-update) | async-done | bytes 786448 | tf_op jit(solution)/shard_map/psum | solution.py:31
  97.0 1.8 fusion.7
  98.8 0.8 fusion.5
  99.6 1.9 fusion.24
  101.5 1.0 fusion.26
  102.8 200.6 %all-reduce.8.cloned.1.call-done = (f32[256,1792]{1,0:T(8,128)}, f32[256,256]{0,1:T(8,128)}) async-done(((f32[256,1792]{1,0:T(8,128)}, f32[256,256]{0,1:T(8,128)}), (f32[256,1792]{1,0:T(8,128)}, f32[256,256]{0,1:T(8,128)})) %all-reduce.8.cloned.1.call-update) | async-done | bytes 2097168 | tf_op jit(solution)/shard_map/psum | solution.py:38
  303.3 1.1 copy.8
  304.4 1.0 fusion.17
  305.4 11.7 %cholesky.49 = f32[128,128]{1,0:T(8,128)S(1)} custom-call(f32[128,128]{1,0:T(8,128)S(1)} %cholesky.115), custom_call_target="Cholesky" | custom-call | tf_op jit(solution)/shard_map/jit(cholesky)/cholesky | solution.py:21
  317.2 9.8 %custom-call.18 = f32[1,128,128]{1,2,0:T(8,128)S(1)} custom-call(f32[1,128,128]{2,1,0:T(8,128)S(1)} %get-tuple-element.31), custom_call_target="InvertDiagBlocksLowerTriangular" | custom-call | tf_op jit(solution)/shard_map/jit(cholesky)/cholesky | solution.py:21
  327.5 11.7 %cholesky.103 = f32[128,128]{1,0:T(8,128)S(1)} custom-call(f32[128,128]{1,0:T(8,128)S(1)} %convolution_subtract_fusion.2), custom_call_target="Cholesky" | custom-call | tf_op jit(solution)/shard_map/jit(cholesky)/cholesky | solution.py:21
  339.2 0.6 compare_reduce_fusion
  341.3 4.2 while.1
  341.5 0.6 fusion.65
  342.0 1.4 bitcast_dynamic-update-slice_fusion.2
  344.0 1.4 bitcast_dynamic-update-slice_fusion.2
  345.4 19.7 %custom-call.19 = f32[2,128,128]{1,2,0:T(8,128)S(1)} custom-call(f32[2,128,128]{2,1,0:T(8,128)S(1)} %get-tuple-element.9), custom_call_target="InvertDiagBlocksLowerTriangular" | custom-call | tf_op jit(solution)/shard_map/jit(_cho_solve)/triangular_solve | solution.py:22
  365.1 2.2 fusion.12
  367.4 0.9 convolution_subtract_fusion.1
  368.3 0.9 fusion.37
  369.3 1.7 fusion.36
  371.0 0.9 convolution_subtract_fusion
  372.0 0.9 fusion.35
  372.9 1.5 convolution_bitcast_fusion
  374.3 2.4 fusion
  376.7 2.6 fusion.1
  379.3 2.7 copy.10
  382.0 72.5 %all-reduce.10.cloned.1.call-done = (f32[512,256]{1,0:T(8,128)}, f32[256,256]{1,0:T(8,128)}) async-done(((f32[512,256]{1,0:T(8,128)}, f32[256,256]{1,0:T(8,128)}), (f32[512,256]{1,0:T(8,128)}, f32[256,256]{1,0:T(8,128)})) %all-reduce.10.cloned.1.call-update) | async-done | bytes 786448 | tf_op jit(solution)/shard_map/psum | solution.py:41
  454.5 1.8 convolution_add_fusion.1
  456.3 1.6 fusion.11
  (41 shorter events, 1.7 us)
Async XLA Ops:
  7.2 6.0 %copy-start = (bf16[512,1792]{1,0:T(8,128)(2,1)S(1)}, bf16[512,1792]{1,0:T(8,128)(2,1)}, u32[]{:S(2)}) copy-start(bf16[512,1792]{1,0:T(8,128)(2,1)} %param.3) | copy-start | bytes 5505028
  7.2 89.8 %all-reduce.12.cloned.1.call-start = ((), (), s32[]{:S(2)}) async-start(), calls=%async_computation.2 | async-start | bytes 1572864 | tf_op jit(solution)/shard_map/psum | solution.py:31
  7.2 6.0 %copy-start.1 = (f32[1792,256]{1,0:T(8,128)S(1)}, f32[1792,256]{1,0:T(8,128)}, u32[]{:S(2)}) copy-start(f32[1792,256]{1,0:T(8,128)} %param.4) | copy-start | bytes 5505028
  13.2 83.8 %copy-start.4 = (f32[512,256]{1,0:T(8,128)S(1)}, f32[512,256]{1,0:T(8,128)}, u32[]{:S(2)}) copy-start(f32[512,256]{1,0:T(8,128)} %param.5) | copy-start | bytes 1572868
  14.7 288.6 %all-reduce.8.cloned.1.call-start = ((), (), s32[]{:S(2)}) async-start(), calls=%async_computation | async-start | bytes 4194304 | tf_op jit(solution)/shard_map/psum | solution.py:38
  97.0 1.8 copy-start.6
  97.0 1.8 copy-start.10
  102.5 352.0 %all-reduce.10.cloned.1.call-start = ((), (), s32[]{:S(2)}) async-start(), calls=%async_computation.1 | async-start | bytes 1572864 | tf_op jit(solution)/shard_map/psum | solution.py:41
  365.1 3.2 copy-start.7
  365.1 2.3 copy-start.3
  371.0 1.0 copy-start.8
  372.9 1.5 copy-start.2
  454.5 1.8 copy-start.5
  454.5 1.8 copy-start.9
Sparse Core Ops, SparseCore 0:
  14.8 82.1 all-reduce.11
  102.6 200.6 all-reduce.7
  376.9 77.5 all-reduce.9
where the time goes:
time: 468 us; the launch traced here: 464 us
  waiting for transfers between devices  355 us (76%)
  other arithmetic  57.2 us (12%)
  matrix products  28.1 us (6%)
  between operations  15.3 us (3%)
  local copies, waits for them, and re-layouts  7.9 us (2%)
    psum x1, waiting for transfers between devices, per_device(): cross, gram_codes = lax.psum((cross_part, gram_part), 'tok')  201 us
    psum x1, waiting for transfers between devices, per_device(): proj, gram_dict = lax.psum((proj_part, self_gram(dictionary)), 'hid')  82.3 us
    psum x1, waiting for transfers between devices, per_device(): proj_two, gram_new = lax.psum((proj_next, self_gram(dict_out)), 'hid')  72.5 us
    another operation x6, other arithmetic, solve_rows(): lower = jnp.linalg.cholesky(gram)  33.9 us
    another operation x3, other arithmetic, solve_rows(): return jax.scipy.linalg.cho_solve((lower, True), cross.T).T  19.7 us
  transfers between devices with their start and end apart: 3, of which 3 were waited for; matrix products, arithmetic and copies ran while one was open for 1% of the time, Pallas kernels for 0%

commit v1 on v0

v1 whole, which is shorter than its diff:
```python
import functools

import jax
import jax.numpy as jnp
from jax import lax
from jax.experimental import pallas as pl
from jax.experimental.pallas import tpu as pltpu
from jax.sharding import PartitionSpec as P

MESH = pl.DeviceIdType.MESH
HIGHEST = lax.Precision.HIGHEST
floor_value = 0.05
XS, YS, ZS = 4, 8, 8
COMP = 256
BLOCK = 16
TN = (((0,), (0,)), ((), ()))
NT = (((1,), (1,)), ((), ()))


def split3(v):
    hi = v.astype(jnp.bfloat16)
    rest = v - hi.astype(jnp.float32)
    mid = rest.astype(jnp.bfloat16)
    low = (rest - mid.astype(jnp.float32)).astype(jnp.bfloat16)
    return hi, mid, low


def outer6(c, y):
    ch, cm, cl = split3(c)
    yh, ym, yl = split3(y)
    lhs = jnp.concatenate([ch, ch, cm, cm, ch, cl], axis=0)
    rhs = jnp.concatenate([yh, ym, yh, ym, yl, yh], axis=0)
    return lax.dot_general(lhs, rhs, TN, preferred_element_type=jnp.float32)


def panel_invert(panel, k):
    size = panel.shape[1]
    tile = jnp.where(k < 128 // BLOCK, panel[:, :128], panel[:, 128:])
    tile = pltpu.roll(tile, lax.rem(128 - lax.rem(k * BLOCK, 128), 128), 1)
    cols = [jnp.broadcast_to(tile[:, j : j + 1], (BLOCK, 128)) for j in range(BLOCK)]
    row = lax.broadcasted_iota(jnp.int32, (BLOCK, 128), 0)
    lane = lax.broadcasted_iota(jnp.int32, (BLOCK, size), 1) - k * BLOCK
    wide_row = lax.broadcasted_iota(jnp.int32, (BLOCK, size), 0)
    for i in range(BLOCK):
        inv = 1.0 / cols[i][i : i + 1, :]
        scaled = cols[i] * inv
        scaled2 = jnp.concatenate([scaled, scaled], axis=1)
        inv2 = jnp.concatenate([inv, inv], axis=1)
        pivot = panel[i : i + 1, :]
        new = jnp.where(wide_row == i, pivot * inv2, panel - scaled2 * pivot)
        panel = jnp.where(lane == i, jnp.where(wide_row == i, inv2, -scaled2), new)
        for j in range(i + 1, BLOCK):
            c = cols[j][i : i + 1, :]
            cols[j] = jnp.where(row == i, c * inv, cols[j] - scaled * c)
    return panel


def invert_blocks(a, first, last):
    size = a.shape[0]

    def body(k, _):
        rows = pl.ds(pl.multiple_of(k * BLOCK, BLOCK), BLOCK)
        panel = a[rows, :]
        lane = lax.broadcasted_iota(jnp.int32, (1, size), 1)
        column = panel * jnp.where(lane < k * BLOCK, -1.0, 1.0)
        new = panel_invert(panel, k)
        inside = (lane >= k * BLOCK) & (lane < k * BLOCK + BLOCK)
        a[...] = jnp.where(inside, 0.0, a[...]) - outer6(column, new)
        a[rows, :] = new
        return 0

    lax.fori_loop(first, last, body, 0)


def update(part, proj, gram, codes):
    both = jnp.concatenate([jnp.maximum(-gram, 0.0), jnp.maximum(gram, 0.0)], axis=0)
    prod = jnp.dot(both, codes, precision=HIGHEST, preferred_element_type=jnp.float32)
    n = gram.shape[0]
    numer = jnp.maximum(proj, 0.0) + prod[:n]
    denom = jnp.maximum(jnp.maximum(-proj, 0.0) + prod[n:], floor_value)
    return part * jnp.sqrt(numer / denom)


def kernel(
    acts, dic, codes, codes_out, dict_out,
    dt, ct, proj, gram, proj_in, gram_in, mid,
    gk, gk_c, gk_x, gk_y, ginv,
    cr, cr_c, cr_x, cr_y, cr_xs, full,
    proj2, gram2, proj2_in, gram2_in, out_t,
    zs, zr, ys, yr, xs, xr, cs, crs,
):
    tok, z = lax.axis_index("tok"), lax.axis_index("hid")
    core, x, y = lax.rem(tok, 2), lax.rem(tok // 2, XS), tok // (2 * XS)

    def at(dx=0, dy=0, dz=0, dc=0):
        px, py = lax.rem(x + dx, XS), lax.rem(y + dy, YS)
        return ((py * XS + px) * 2 + lax.rem(core + dc, 2), lax.rem(z + dz, ZS))

    zorder = (4, 3, 5, 2, 6, 1, 7)
    xorder = (2, 1, 3)

    barrier = pltpu.get_barrier_semaphore()
    partners = [at(dz=o) for o in zorder] + [at(dy=o) for o in zorder] + [at(dx=o) for o in xorder] + [at(dc=1)]
    for p in partners:
        pl.semaphore_signal(barrier, inc=1, device_id=p, device_id_type=MESH)

    def push(src, dst, ss, rs, dev):
        c = pltpu.make_async_remote_copy(
            src_ref=src, dst_ref=dst, send_sem=ss, recv_sem=rs, device_id=dev, device_id_type=MESH
        )
        c.start()
        return c

    def rows(i, n):
        return pl.ds(pl.multiple_of(i * n, n), n)

    n = COMP // ZS

    def scatter_z(part, slots, sem):
        out = []
        for o in zorder:
            dev = at(dz=o)
            out.append(push(part.at[rows(dev[1], n)], slots.at[o - 1], zs.at[sem, o - 1], zr.at[sem, o - 1], dev))
        return out

    def gather_z(buf, sem):
        own = buf.at[rows(z, n)]
        return [push(own, own, zs.at[sem, o - 1], zr.at[sem, o - 1], at(dz=o)) for o in zorder]

    def finish(copies):
        for c in copies:
            c.wait()

    dt[...] = dic[...].T
    proj[...] = lax.dot_general(dt[...].astype(jnp.bfloat16), acts[...], NT, preferred_element_type=jnp.float32)
    pl.semaphore_wait(barrier, len(partners))
    sent = scatter_z(proj, proj_in, 0)
    gram[...] = lax.dot_general(dt[...], dt[...], NT, precision=HIGHEST, preferred_element_type=jnp.float32)
    sent_gram = scatter_z(gram, gram_in, 1)
    ct[...] = codes[...].T
    own = rows(z, n)
    finish(sent)
    proj_sum = proj[own, :] + sum(proj_in[i] for i in range(ZS - 1))
    finish(sent_gram)
    gram_sum = gram[own, :] + sum(gram_in[i] for i in range(ZS - 1))
    mid[own, :] = update(ct[own, :], proj_sum, gram_sum, ct[...])
    finish(gather_z(mid, 2))

    low = mid[...].astype(jnp.bfloat16)
    gk[...] = lax.dot_general(low, low, NT, preferred_element_type=jnp.float32)
    half = COMP // 2
    g_core = push(gk.at[rows(1 - core, half)], gk_c, cs.at[0], crs.at[0], at(dc=1))
    tiles = acts.shape[1] // 128
    for j in range(0, tiles, 2):
        block = jnp.dot(low, acts[:, j * 128 : j * 128 + 256], preferred_element_type=jnp.float32)
        for i in (j, j + 1):
            cr[i // (tiles // 2), pl.ds((i % (tiles // 2)) * COMP, COMP), :] = block[:, (i - j) * 128 : (i - j + 1) * 128]
    c_core = push(cr.at[1 - core], cr_c, cs.at[1], crs.at[1], at(dc=1))
    g_core.wait()
    gk_c[...] += gk[rows(core, half), :]
    quarter = half // XS
    g_x = []
    for o in xorder:
        px = lax.rem(x + o, XS)
        g_x.append(push(gk_c.at[rows(px, quarter)], gk_x.at[o - 1], xs.at[0, o - 1], xr.at[0, o - 1], at(dx=o)))
    c_core.wait()
    cr_c[...] += cr[core]
    span = cr_c.shape[0] // XS
    c_x = []
    for o in xorder:
        px = lax.rem(x + o, XS)
        c_x.append(push(cr_c.at[rows(px, span)], cr_x.at[o - 1], xs.at[1, o - 1], xr.at[1, o - 1], at(dx=o)))
    finish(g_x)
    gk_y[y] = gk_c[rows(x, quarter), :] + gk_x[0] + gk_x[1] + gk_x[2]
    g_y = [push(gk_y.at[y], gk_y.at[y], ys.at[0, o - 1], yr.at[0, o - 1], at(dy=o)) for o in zorder]
    finish(g_y)
    place = core * XS + x
    ginv[rows(place, quarter), :] = sum(gk_y[i] for i in range(YS))
    spot = ginv.at[rows(place, quarter)]
    g_x2 = [push(spot, spot, xs.at[2, o - 1], xr.at[2, o - 1], at(dx=o)) for o in xorder]
    finish(c_x)
    cr_xs[...] = cr_c[rows(x, span), :] + cr_x[0] + cr_x[1] + cr_x[2]
    piece = span // YS
    c_y = []
    for o in zorder:
        py = lax.rem(y + o, YS)
        c_y.append(push(cr_xs.at[rows(py, piece)], cr_y.at[o - 1], ys.at[1, o - 1], yr.at[1, o - 1], at(dy=o)))
    finish(g_x2)
    spot = ginv.at[rows(core, half)]
    push(spot, spot, cs.at[2], crs.at[2], at(dc=1)).wait()

    steps = COMP // BLOCK
    invert_blocks(ginv, 0, steps // 2)
    finish(c_y)
    spot = full.at[core, rows(x * YS + y, piece)]
    spot[...] = cr_xs[rows(y, piece), :] + sum(cr_y[i] for i in range(YS - 1))
    c_y2 = [push(spot, spot, ys.at[2, o - 1], yr.at[2, o - 1], at(dy=o)) for o in zorder]
    invert_blocks(ginv, steps // 2, steps)
    finish(c_y2)
    spot = full.at[core, rows(x, span)]
    finish([push(spot, spot, xs.at[3, o - 1], xr.at[3, o - 1], at(dx=o)) for o in xorder])
    spot = full.at[core]
    push(spot, spot, cs.at[3], crs.at[3], at(dc=1)).wait()

    for j in range(0, tiles, 2):
        pair = [full[i // (tiles // 2), pl.ds((i % (tiles // 2)) * COMP, COMP), :] for i in (j, j + 1)]
        block = jnp.concatenate(pair, axis=1)
        dt[:, j * 128 : j * 128 + 256] = jnp.dot(
            ginv[...], block, precision=HIGHEST, preferred_element_type=jnp.float32
        )
    proj2[...] = lax.dot_general(dt[...].astype(jnp.bfloat16), acts[...], NT, preferred_element_type=jnp.float32)
    sent = scatter_z(proj2, proj2_in, 3)
    gram2[...] = lax.dot_general(dt[...], dt[...], NT, precision=HIGHEST, preferred_element_type=jnp.float32)
    sent_gram = scatter_z(gram2, gram2_in, 4)
    dict_out[...] = dt[...].T
    finish(sent)
    proj_sum = proj2[own, :] + sum(proj2_in[i] for i in range(ZS - 1))
    finish(sent_gram)
    gram_sum = gram2[own, :] + sum(gram2_in[i] for i in range(ZS - 1))
    out_t[own, :] = update(mid[own, :], proj_sum, gram_sum, mid[...])
    finish(gather_z(out_t, 5))
    codes_out[...] = out_t[...].T


def per_device(acts, dictionary, codes):
    tokens, hid = acts.shape
    f32 = jnp.float32
    v = lambda *s: pltpu.VMEM(s, f32)
    n = COMP // ZS
    half = hid * COMP // 2 // 128
    vmem = pl.BlockSpec(memory_space=pltpu.VMEM)
    dma = pltpu.SemaphoreType.DMA
    return pl.pallas_call(
        kernel,
        name="semi_nmf",
        out_shape=(jax.ShapeDtypeStruct((tokens, COMP), f32), jax.ShapeDtypeStruct((hid, COMP), f32)),
        in_specs=[vmem] * 3,
        out_specs=(vmem, vmem),
        scratch_shapes=[
            v(COMP, hid), v(COMP, tokens), v(COMP, tokens), v(COMP, COMP),
            v(ZS - 1, n, tokens), v(ZS - 1, n, COMP), v(COMP, tokens),
            v(COMP, COMP), v(COMP // 2, COMP), v(XS - 1, COMP // 2 // XS, COMP), v(YS, COMP // 2 // XS, COMP),
            v(COMP, COMP),
            v(2, half, 128), v(half, 128), v(XS - 1, half // XS, 128), v(YS - 1, half // XS // YS, 128),
            v(half // XS, 128), v(2, half, 128),
            v(COMP, tokens), v(COMP, COMP), v(ZS - 1, n, tokens), v(ZS - 1, n, COMP), v(COMP, tokens),
            dma((6, ZS - 1)), dma((6, ZS - 1)), dma((3, YS - 1)), dma((3, YS - 1)),
            dma((4, XS - 1)), dma((4, XS - 1)), dma((4,)), dma((4,)),
        ],
        compiler_params=pltpu.CompilerParams(
            collective_id=0, has_side_effects=True, vmem_limit_bytes=56 * 1024 * 1024
        ),
    )(acts, dictionary, codes)


def solution(mesh):
    return jax.shard_map(
        per_device,
        mesh=mesh,
        in_specs=(P("tok", "hid"), P("hid", None), P("tok", None)),
        out_specs=(P("tok", None), P("hid", None)),
        check_vma=False,
    )
```

time: 468 us -> 139 us (0.30)
  waiting for transfers between devices: 355 us -> 0 us
  Pallas kernels: 0 us -> 134 us
  other arithmetic: 57.2 us -> 0 us
  matrix products: 28.1 us -> 0 us
  between operations: 15.3 us -> 0.64 us
    psum x3 -> x0, waiting for transfers between devices: 355 us -> none  [the longest x1 201 us: per_device(): cross, gram_codes = lax.psum((cross_part, gram_part), 'tok')]
    pallas_call x0 -> x1, Pallas kernels: none -> 134 us  [per_device(): pl.pallas_call(kernel, name='semi_nmf', out_shape=(jax.ShapeDtypeStruct((...]
    another operation x9 -> x0, other arithmetic: 53.7 us -> none  [the longest x6 33.9 us: solve_rows(): lower = jnp.linalg.cholesky(gram)]
    dot_general x10 -> x0, matrix products: 20 us -> none  [the longest x2 8.33 us: self_gram(): return jnp.dot(matrix.T, matrix, precision=lax.Precision.HIGHEST)]
    another operation x8 -> x0, matrix products: 8.1 us -> none  [the longest x6 7.62 us: solve_rows(): return jax.scipy.linalg.cho_solve((lower, True), cross.T).T]
  transfers between devices with their start and end apart: 3 -> 0, of which waited for: 3 -> 0; matrix products, arithmetic and copies ran while one was open for 1% -> 0% of each run, Pallas kernels for 0% -> 0%
where the time goes in v1:
time: 139 us
  Pallas kernels  134 us (96%)
  local copies, waits for them, and re-layouts  4.71 us (3%)
    pallas_call x1, Pallas kernels, per_device(): pl.pallas_call(kernel, name='semi_nmf', out_shape=(jax.ShapeDtypeStruct((...  134 us
    unnamed x2, local copies, waits for them, and re-layouts  4.71 us

profile of v1, /device:TPU:1, one launch (start us, length us, event | category | flops | bytes accessed | tf_op | source)
XLA Modules:
  0.0 139.1 jit_solution(2659988211296518945)
XLA Ops:
  0.6 133.7 %semi_nmf.1 = (f32[512,256]{1,0:T(8,128)}, f32[1792,256]{1,0:T(8,128)}) custom-call(bf16[512,1792]{1,0:T(8,128)(2,1)} %acts.1, f32[1792,256]{1,0:T(8,128)} %dic.1, f32[512,256]{1,0:T(8,128)} %codes.1), custom_call_target="tpu_custom_call" | custom-call | tf_op jit(solution)/shard_map/semi_nmf/pallas_call | solution.py:233
  134.4 1.9 %copy.7 = f32[512,256]{1,0:T(8,128)} copy(f32[512,256]{1,0:T(8,128)} %get-tuple-element.4) | data formatting | bytes 1048576
  136.2 2.8 %copy.8 = f32[1792,256]{1,0:T(8,128)} copy(f32[1792,256]{1,0:T(8,128)} %get-tuple-element.5) | data formatting | bytes 3670016

commit v2 on v1

--- a/solution.py
+++ b/solution.py
@@ -82,11 +82,11 @@
 
 
 def kernel(
-    acts, dic, codes, codes_out, dict_out,
-    dt, ct, proj, gram, proj_in, gram_in, mid,
+    acts, dic, codes, out_t, dict_out,
+    dt, ct, proj, gram, proj_in, gram_in, gram_tiles, mid,
     gk, gk_c, gk_x, gk_y, ginv,
     cr, cr_c, cr_x, cr_y, cr_xs, full,
-    proj2, gram2, proj2_in, gram2_in, out_t,
+    proj2, gram2, proj2_in, gram2_in, gram2_tiles,
     zs, zr, ys, yr, xs, xr, cs, crs,
 ):
     tok, z = lax.axis_index("tok"), lax.axis_index("hid")
@@ -127,6 +127,27 @@
         own = buf.at[rows(z, n)]
         return [push(own, own, zs.at[sem, o - 1], zr.at[sem, o - 1], at(dz=o)) for o in zorder]
 
+    def send_gram(matrix, part, slots, sem):
+        picked = [matrix[pl.ds(pl.multiple_of(j * n + x * 8, 8), 8), :] for j in range(ZS)]
+        part[...] = lax.dot_general(
+            jnp.concatenate(picked, axis=0), matrix[rows(core, 128), :], NT,
+            precision=HIGHEST, preferred_element_type=jnp.float32,
+        ).reshape(part.shape)
+        out = []
+        for o in zorder:
+            dev = at(dz=o)
+            out.append(push(part.at[dev[1]], slots.at[o - 1], zs.at[sem, o - 1], zr.at[sem, o - 1], dev))
+        return out
+
+    def share_gram(sent, part, slots, tiles, step):
+        finish(sent)
+        spot = tiles.at[core, x]
+        spot[...] = part[z] + sum(slots[i] for i in range(ZS - 1))
+        finish([push(spot, spot, xs.at[step, o - 1], xr.at[step, o - 1], at(dx=o)) for o in xorder])
+        spot = tiles.at[core]
+        push(spot, spot, cs.at[step], crs.at[step], at(dc=1)).wait()
+        return jnp.concatenate([tiles[i].reshape(n, 128) for i in range(2)], axis=1)
+
     def finish(copies):
         for c in copies:
             c.wait()
@@ -134,15 +155,13 @@
     dt[...] = dic[...].T
     proj[...] = lax.dot_general(dt[...].astype(jnp.bfloat16), acts[...], NT, preferred_element_type=jnp.float32)
     pl.semaphore_wait(barrier, len(partners))
+    sent_gram = send_gram(dt, gram, gram_in, 1)
     sent = scatter_z(proj, proj_in, 0)
-    gram[...] = lax.dot_general(dt[...], dt[...], NT, precision=HIGHEST, preferred_element_type=jnp.float32)
-    sent_gram = scatter_z(gram, gram_in, 1)
     ct[...] = codes[...].T
     own = rows(z, n)
+    gram_sum = share_gram(sent_gram, gram, gram_in, gram_tiles, 4)
     finish(sent)
     proj_sum = proj[own, :] + sum(proj_in[i] for i in range(ZS - 1))
-    finish(sent_gram)
-    gram_sum = gram[own, :] + sum(gram_in[i] for i in range(ZS - 1))
     mid[own, :] = update(ct[own, :], proj_sum, gram_sum, ct[...])
     finish(gather_z(mid, 2))
 
@@ -208,18 +227,29 @@
         dt[:, j * 128 : j * 128 + 256] = jnp.dot(
             ginv[...], block, precision=HIGHEST, preferred_element_type=jnp.float32
         )
+    sent_gram = send_gram(dt, gram2, gram2_in, 4)
     proj2[...] = lax.dot_general(dt[...].astype(jnp.bfloat16), acts[...], NT, preferred_element_type=jnp.float32)
     sent = scatter_z(proj2, proj2_in, 3)
-    gram2[...] = lax.dot_general(dt[...], dt[...], NT, precision=HIGHEST, preferred_element_type=jnp.float32)
-    sent_gram = scatter_z(gram2, gram2_in, 4)
     dict_out[...] = dt[...].T
+    gram_sum = share_gram(sent_gram, gram2, gram2_in, gram2_tiles, 5)
     finish(sent)
     proj_sum = proj2[own, :] + sum(proj2_in[i] for i in range(ZS - 1))
-    finish(sent_gram)
-    gram_sum = gram2[own, :] + sum(gram2_in[i] for i in range(ZS - 1))
     out_t[own, :] = update(mid[own, :], proj_sum, gram_sum, mid[...])
     finish(gather_z(out_t, 5))
+
+
+def leave(out_t, dict_in, codes_out, dict_out, sem):
+    parts = 4
+    step = dict_in.shape[0] // parts
+    copies = []
+    for i in range(parts):
+        spot = pl.ds(i * step, step)
+        copies.append(pltpu.make_async_copy(dict_in.at[spot], dict_out.at[spot], sem.at[i]))
+    for c in copies:
+        c.start()
     codes_out[...] = out_t[...].T
+    for c in copies:
+        c.wait()
 
 
 def per_device(acts, dictionary, codes):
@@ -230,27 +260,37 @@
     half = hid * COMP // 2 // 128
     vmem = pl.BlockSpec(memory_space=pltpu.VMEM)
     dma = pltpu.SemaphoreType.DMA
-    return pl.pallas_call(
+    out_t, dict_new = pl.pallas_call(
         kernel,
         name="semi_nmf",
-        out_shape=(jax.ShapeDtypeStruct((tokens, COMP), f32), jax.ShapeDtypeStruct((hid, COMP), f32)),
+        out_shape=(jax.ShapeDtypeStruct((COMP, tokens), f32), jax.ShapeDtypeStruct((hid, COMP), f32)),
         in_specs=[vmem] * 3,
         out_specs=(vmem, vmem),
         scratch_shapes=[
-            v(COMP, hid), v(COMP, tokens), v(COMP, tokens), v(COMP, COMP),
-            v(ZS - 1, n, tokens), v(ZS - 1, n, COMP), v(COMP, tokens),
+            v(COMP, hid), v(COMP, tokens), v(COMP, tokens), v(ZS, 8, 128),
+            v(ZS - 1, n, tokens), v(ZS - 1, 8, 128), v(2, XS, 8, 128), v(COMP, tokens),
             v(COMP, COMP), v(COMP // 2, COMP), v(XS - 1, COMP // 2 // XS, COMP), v(YS, COMP // 2 // XS, COMP),
             v(COMP, COMP),
             v(2, half, 128), v(half, 128), v(XS - 1, half // XS, 128), v(YS - 1, half // XS // YS, 128),
             v(half // XS, 128), v(2, half, 128),
-            v(COMP, tokens), v(COMP, COMP), v(ZS - 1, n, tokens), v(ZS - 1, n, COMP), v(COMP, tokens),
+            v(COMP, tokens), v(ZS, 8, 128), v(ZS - 1, n, tokens), v(ZS - 1, 8, 128), v(2, XS, 8, 128),
             dma((6, ZS - 1)), dma((6, ZS - 1)), dma((3, YS - 1)), dma((3, YS - 1)),
-            dma((4, XS - 1)), dma((4, XS - 1)), dma((4,)), dma((4,)),
+            dma((6, XS - 1)), dma((6, XS - 1)), dma((6,)), dma((6,)),
         ],
         compiler_params=pltpu.CompilerParams(
             collective_id=0, has_side_effects=True, vmem_limit_bytes=56 * 1024 * 1024
         ),
     )(acts, dictionary, codes)
+    anywhere = pl.BlockSpec(memory_space=pl.ANY)
+    return pl.pallas_call(
+        leave,
+        name="leave",
+        out_shape=(jax.ShapeDtypeStruct((tokens, COMP), f32), jax.ShapeDtypeStruct((hid, COMP), f32)),
+        in_specs=[vmem, anywhere],
+        out_specs=(vmem, anywhere),
+        scratch_shapes=[dma((4,))],
+        compiler_params=pltpu.CompilerParams(vmem_limit_bytes=56 * 1024 * 1024),
+    )(out_t, dict_new)
 
 
 def solution(mesh):

time: 139 us -> 186 us (1.34)
  Pallas kernels: 134 us -> 185 us
  local copies, waits for them, and re-layouts: 4.71 us -> 0 us
    pallas_call x0 -> x1, Pallas kernels: none -> 58.6 us  [per_device(): pl.pallas_call(leave, name='leave', out_shape=(jax.ShapeDtypeStruct((toke...]
    pallas_call x1, Pallas kernels: 134 us -> 127 us  [per_device(): pl.pallas_call(kernel, name='semi_nmf', out_shape=(jax.ShapeDtypeStruct((...]
    unnamed x2 -> x0, local copies, waits for them, and re-layouts: 4.71 us -> none
where the time goes in v2:
time: 186 us
  Pallas kernels  185 us (99%)
    pallas_call x1, Pallas kernels, per_device(): pl.pallas_call(kernel, name='semi_nmf', out_shape=(jax.ShapeDtypeStruct((...  127 us
    pallas_call x1, Pallas kernels, per_device(): pl.pallas_call(leave, name='leave', out_shape=(jax.ShapeDtypeStruct((toke...  58.6 us

profile of v2, /device:TPU:1, one launch (start us, length us, event | category | flops | bytes accessed | tf_op | source)
XLA Modules:
  0.0 185.7 jit_solution(830694479700827804)
XLA Ops:
  0.6 126.5 %semi_nmf.1 = (f32[256,512]{1,0:T(8,128)}, f32[1792,256]{1,0:T(8,128)}) custom-call(bf16[512,1792]{1,0:T(8,128)(2,1)} %acts.1, f32[1792,256]{1,0:T(8,128)} %dic.1, f32[512,256]{1,0:T(8,128)} %codes.1), custom_call_target="tpu_custom_call" | custom-call | tf_op jit(solution)/shard_map/semi_nmf/pallas_call | solution.py:263
  127.1 58.6 %leave.1 = (f32[512,256]{1,0:T(8,128)}, f32[1792,256]{1,0:T(8,128)}) custom-call(f32[256,512]{1,0:T(8,128)} %get-tuple-element.4.out_t, f32[1792,256]{1,0:T(8,128)} %get-tuple-element.5.dict_in), custom_call_target="tpu_custom_call" | custom-call | tf_op jit(solution)/shard_map/leave/pallas_call | solution.py:285

commit v3 on v2

--- a/solution.py
+++ b/solution.py
@@ -84,8 +84,8 @@
 def kernel(
     acts, dic, codes, out_t, dict_out,
     dt, ct, proj, gram, proj_in, gram_in, gram_tiles, mid,
-    gk, gk_c, gk_x, gk_y, ginv,
-    cr, cr_c, cr_x, cr_y, cr_xs, full,
+    gk, gk_c, gk_x, gk_y, gk_z, ginv,
+    cr, cr_c, cr_x0, cr_s0, cr_y0, cr_y1, cr_s1, cr_x1, full,
     proj2, gram2, proj2_in, gram2_in, gram2_tiles,
     zs, zr, ys, yr, xs, xr, cs, crs,
 ):
@@ -166,67 +166,108 @@
     finish(gather_z(mid, 2))
 
     low = mid[...].astype(jnp.bfloat16)
-    gk[...] = lax.dot_general(low, low, NT, preferred_element_type=jnp.float32)
-    half = COMP // 2
-    g_core = push(gk.at[rows(1 - core, half)], gk_c, cs.at[0], crs.at[0], at(dc=1))
-    tiles = acts.shape[1] // 128
-    for j in range(0, tiles, 2):
-        block = jnp.dot(low, acts[:, j * 128 : j * 128 + 256], preferred_element_type=jnp.float32)
-        for i in (j, j + 1):
-            cr[i // (tiles // 2), pl.ds((i % (tiles // 2)) * COMP, COMP), :] = block[:, (i - j) * 128 : (i - j + 1) * 128]
-    c_core = push(cr.at[1 - core], cr_c, cs.at[1], crs.at[1], at(dc=1))
-    g_core.wait()
-    gk_c[...] += gk[rows(core, half), :]
-    quarter = half // XS
-    g_x = []
+    low_own = mid[own, :].astype(jnp.bfloat16)
+    gk[...] = lax.dot_general(low_own, low, NT, preferred_element_type=jnp.float32).reshape(gk.shape)
+    g_c = push(gk.at[1 - core], gk_c, cs.at[0], crs.at[0], at(dc=1))
+
+    halftiles = acts.shape[1] // 256
+    part0 = halftiles - halftiles // 3
+    cut = part0 * COMP
+    rest = halftiles * COMP - cut
+
+    def cross(which, first, last):
+        for j in range(first, last):
+            lanes = pl.ds(pl.multiple_of((which * halftiles + j) * 128, 128), 128)
+            cr[which, pl.ds(j * COMP, COMP), :] = jnp.dot(low, acts[:, lanes], preferred_element_type=jnp.float32)
+
+    head, tail = pl.ds(0, cut), pl.ds(cut, rest)
+    cross(1 - core, 0, part0)
+    c_c0 = push(cr.at[1 - core, head], cr_c.at[head], cs.at[1], crs.at[1], at(dc=1))
+    cross(1 - core, part0, halftiles)
+    c_c1 = push(cr.at[1 - core, tail], cr_c.at[tail], cs.at[2], crs.at[2], at(dc=1))
+    g_c.wait()
+    gk_x[x] = gk[core] + gk_c[...]
+    g_x = [push(gk_x.at[x], gk_x.at[x], xs.at[0, o - 1], xr.at[0, o - 1], at(dx=o)) for o in xorder]
+    cross(core, 0, halftiles)
+    c_c0.wait()
+    cr_c[head, :] += cr[core, head, :]
+    xspan, xpiece = cut // XS, cut // XS // YS
+    yspan, ypiece = rest // YS, rest // YS // XS
+
+    def tail_rows(i, size):
+        return pl.ds(pl.multiple_of(cut + i * size, size), size)
+
+    c0 = []
     for o in xorder:
         px = lax.rem(x + o, XS)
-        g_x.append(push(gk_c.at[rows(px, quarter)], gk_x.at[o - 1], xs.at[0, o - 1], xr.at[0, o - 1], at(dx=o)))
-    c_core.wait()
-    cr_c[...] += cr[core]
-    span = cr_c.shape[0] // XS
-    c_x = []
+        c0.append(push(cr_c.at[rows(px, xspan)], cr_x0.at[o - 1], xs.at[1, o - 1], xr.at[1, o - 1], at(dx=o)))
+    finish(g_x)
+    gk_y[y] = sum(gk_x[i] for i in range(XS))
+    g_y = [push(gk_y.at[y], gk_y.at[y], ys.at[0, o - 1], yr.at[0, o - 1], at(dy=o)) for o in zorder]
+    c_c1.wait()
+    cr_c[tail, :] += cr[core, tail, :]
+    c1 = []
+    for o in zorder:
+        py = lax.rem(y + o, YS)
+        c1.append(push(cr_c.at[tail_rows(py, yspan)], cr_y1.at[o - 1], ys.at[1, o - 1], yr.at[1, o - 1], at(dy=o)))
+    finish(g_y)
+    spot = gk_z.at[z, core]
+    spot[...] = sum(gk_y[i] for i in range(YS))
+    g_z = [push(spot, spot, zs.at[6, o - 1], zr.at[6, o - 1], at(dz=o)) for o in zorder]
+    finish(c0)
+    cr_s0[...] = cr_c[rows(x, xspan), :] + cr_x0[0] + cr_x0[1] + cr_x0[2]
+    c0 = []
+    for o in zorder:
+        py = lax.rem(y + o, YS)
+        c0.append(push(cr_s0.at[rows(py, xpiece)], cr_y0.at[o - 1], ys.at[2, o - 1], yr.at[2, o - 1], at(dy=o)))
+    finish(c1)
+    cr_s1[...] = cr_c[tail_rows(y, yspan), :] + sum(cr_y1[i] for i in range(YS - 1))
+    c1 = []
     for o in xorder:
         px = lax.rem(x + o, XS)
-        c_x.append(push(cr_c.at[rows(px, span)], cr_x.at[o - 1], xs.at[1, o - 1], xr.at[1, o - 1], at(dx=o)))
-    finish(g_x)
-    gk_y[y] = gk_c[rows(x, quarter), :] + gk_x[0] + gk_x[1] + gk_x[2]
-    g_y = [push(gk_y.at[y], gk_y.at[y], ys.at[0, o - 1], yr.at[0, o - 1], at(dy=o)) for o in zorder]
-    finish(g_y)
-    place = core * XS + x
-    ginv[rows(place, quarter), :] = sum(gk_y[i] for i in range(YS))
-    spot = ginv.at[rows(place, quarter)]
-    g_x2 = [push(spot, spot, xs.at[2, o - 1], xr.at[2, o - 1], at(dx=o)) for o in xorder]
-    finish(c_x)
-    cr_xs[...] = cr_c[rows(x, span), :] + cr_x[0] + cr_x[1] + cr_x[2]
-    piece = span // YS
-    c_y = []
-    for o in zorder:
-        py = lax.rem(y + o, YS)
-        c_y.append(push(cr_xs.at[rows(py, piece)], cr_y.at[o - 1], ys.at[1, o - 1], yr.at[1, o - 1], at(dy=o)))
-    finish(g_x2)
-    spot = ginv.at[rows(core, half)]
-    push(spot, spot, cs.at[2], crs.at[2], at(dc=1)).wait()
+        c1.append(push(cr_s1.at[rows(px, ypiece)], cr_x1.at[o - 1], xs.at[2, o - 1], xr.at[2, o - 1], at(dx=o)))
+    finish(c1)
+    spot = full.at[core, tail_rows(y * XS + x, ypiece)]
+    spot[...] = cr_s1[rows(x, ypiece), :] + cr_x1[0] + cr_x1[1] + cr_x1[2]
+    c1 = [push(spot, spot, xs.at[3, o - 1], xr.at[3, o - 1], at(dx=o)) for o in xorder]
+    finish(g_z)
+    spot = gk_z.at[:, core]
+    g_c = push(spot, spot, cs.at[3], crs.at[3], at(dc=1))
+    finish(c0)
+    spot = full.at[core, rows(x * YS + y, xpiece)]
+    spot[...] = cr_s0[rows(y, xpiece), :] + sum(cr_y0[i] for i in range(YS - 1))
+    c0 = [push(spot, spot, ys.at[3, o - 1], yr.at[3, o - 1], at(dy=o)) for o in zorder]
+    finish(c1)
+    spot = full.at[core, tail_rows(y, yspan)]
+    c1 = [push(spot, spot, ys.at[4, o - 1], yr.at[4, o - 1], at(dy=o)) for o in zorder]
+    g_c.wait()
+    ginv[...] = gk_z[...].reshape(COMP, COMP)
 
     steps = COMP // BLOCK
     invert_blocks(ginv, 0, steps // 2)
-    finish(c_y)
-    spot = full.at[core, rows(x * YS + y, piece)]
-    spot[...] = cr_xs[rows(y, piece), :] + sum(cr_y[i] for i in range(YS - 1))
-    c_y2 = [push(spot, spot, ys.at[2, o - 1], yr.at[2, o - 1], at(dy=o)) for o in zorder]
+    finish(c0)
+    spot = full.at[core, rows(x, xspan)]
+    c0 = [push(spot, spot, xs.at[6, o - 1], xr.at[6, o - 1], at(dx=o)) for o in xorder]
+    finish(c1)
+    spot = full.at[core, tail]
+    c1 = push(spot, spot, cs.at[6], crs.at[6], at(dc=1))
     invert_blocks(ginv, steps // 2, steps)
-    finish(c_y2)
-    spot = full.at[core, rows(x, span)]
-    finish([push(spot, spot, xs.at[3, o - 1], xr.at[3, o - 1], at(dx=o)) for o in xorder])
-    spot = full.at[core]
-    push(spot, spot, cs.at[3], crs.at[3], at(dc=1)).wait()
-
-    for j in range(0, tiles, 2):
-        pair = [full[i // (tiles // 2), pl.ds((i % (tiles // 2)) * COMP, COMP), :] for i in (j, j + 1)]
-        block = jnp.concatenate(pair, axis=1)
-        dt[:, j * 128 : j * 128 + 256] = jnp.dot(
-            ginv[...], block, precision=HIGHEST, preferred_element_type=jnp.float32
-        )
+    finish(c0)
+    spot = full.at[core, head]
+    c0 = push(spot, spot, cs.at[7], crs.at[7], at(dc=1))
+
+    def solve(first, last):
+        for j in range(first, last):
+            span = pl.ds(j * COMP, COMP)
+            block = jnp.concatenate([full[0, span, :], full[1, span, :]], axis=1)
+            solved = jnp.dot(ginv[...], block, precision=HIGHEST, preferred_element_type=jnp.float32)
+            for i in range(2):
+                dt[:, (i * halftiles + j) * 128 : (i * halftiles + j + 1) * 128] = solved[:, i * 128 : i * 128 + 128]
+
+    c1.wait()
+    solve(part0, halftiles)
+    c0.wait()
+    solve(0, part0)
     sent_gram = send_gram(dt, gram2, gram2_in, 4)
     proj2[...] = lax.dot_general(dt[...].astype(jnp.bfloat16), acts[...], NT, preferred_element_type=jnp.float32)
     sent = scatter_z(proj2, proj2_in, 3)
@@ -238,17 +279,25 @@
     finish(gather_z(out_t, 5))
 
 
-def leave(out_t, dict_in, codes_out, dict_out, sem):
+def leave(out_t, dict_in, codes_out, dict_out, held_t, held_codes, held_dict, ins, outs):
     parts = 4
     step = dict_in.shape[0] // parts
-    copies = []
-    for i in range(parts):
-        spot = pl.ds(i * step, step)
-        copies.append(pltpu.make_async_copy(dict_in.at[spot], dict_out.at[spot], sem.at[i]))
-    for c in copies:
+    spots = [pl.ds(i * step, step) for i in range(parts)]
+    first = pltpu.make_async_copy(out_t, held_t, ins.at[parts])
+    first.start()
+    arriving = [pltpu.make_async_copy(dict_in.at[p], held_dict.at[p], ins.at[i]) for i, p in enumerate(spots)]
+    for c in arriving:
         c.start()
-    codes_out[...] = out_t[...].T
-    for c in copies:
+    leaving = []
+    for i, p in enumerate(spots):
+        arriving[i].wait()
+        leaving.append(pltpu.make_async_copy(held_dict.at[p], dict_out.at[p], outs.at[i]))
+        leaving[-1].start()
+    first.wait()
+    held_codes[...] = held_t[...].T
+    leaving.append(pltpu.make_async_copy(held_codes, codes_out, outs.at[parts]))
+    leaving[-1].start()
+    for c in leaving:
         c.wait()
 
 
@@ -258,6 +307,8 @@
     v = lambda *s: pltpu.VMEM(s, f32)
     n = COMP // ZS
     half = hid * COMP // 2 // 128
+    cut = (hid // 256 - hid // 256 // 3) * COMP
+    rest = half - cut
     vmem = pl.BlockSpec(memory_space=pltpu.VMEM)
     dma = pltpu.SemaphoreType.DMA
     out_t, dict_new = pl.pallas_call(
@@ -269,13 +320,13 @@
         scratch_shapes=[
             v(COMP, hid), v(COMP, tokens), v(COMP, tokens), v(ZS, 8, 128),
             v(ZS - 1, n, tokens), v(ZS - 1, 8, 128), v(2, XS, 8, 128), v(COMP, tokens),
-            v(COMP, COMP), v(COMP // 2, COMP), v(XS - 1, COMP // 2 // XS, COMP), v(YS, COMP // 2 // XS, COMP),
+            v(2, n // 2, COMP), v(n // 2, COMP), v(XS, n // 2, COMP), v(YS, n // 2, COMP), v(ZS, 2, n // 2, COMP),
             v(COMP, COMP),
-            v(2, half, 128), v(half, 128), v(XS - 1, half // XS, 128), v(YS - 1, half // XS // YS, 128),
-            v(half // XS, 128), v(2, half, 128),
+            v(2, half, 128), v(half, 128), v(XS - 1, cut // XS, 128), v(cut // XS, 128), v(YS - 1, cut // XS // YS, 128),
+            v(YS - 1, rest // YS, 128), v(rest // YS, 128), v(XS - 1, rest // YS // XS, 128), v(2, half, 128),
             v(COMP, tokens), v(ZS, 8, 128), v(ZS - 1, n, tokens), v(ZS - 1, 8, 128), v(2, XS, 8, 128),
-            dma((6, ZS - 1)), dma((6, ZS - 1)), dma((3, YS - 1)), dma((3, YS - 1)),
-            dma((6, XS - 1)), dma((6, XS - 1)), dma((6,)), dma((6,)),
+            dma((7, ZS - 1)), dma((7, ZS - 1)), dma((5, YS - 1)), dma((5, YS - 1)),
+            dma((7, XS - 1)), dma((7, XS - 1)), dma((8,)), dma((8,)),
         ],
         compiler_params=pltpu.CompilerParams(
             collective_id=0, has_side_effects=True, vmem_limit_bytes=56 * 1024 * 1024
@@ -286,9 +337,9 @@
         leave,
         name="leave",
         out_shape=(jax.ShapeDtypeStruct((tokens, COMP), f32), jax.ShapeDtypeStruct((hid, COMP), f32)),
-        in_specs=[vmem, anywhere],
-        out_specs=(vmem, anywhere),
-        scratch_shapes=[dma((4,))],
+        in_specs=[anywhere] * 2,
+        out_specs=(anywhere, anywhere),
+        scratch_shapes=[v(COMP, tokens), v(tokens, COMP), v(hid, COMP), dma((5,)), dma((5,))],
         compiler_params=pltpu.CompilerParams(vmem_limit_bytes=56 * 1024 * 1024),
     )(out_t, dict_new)
 

time: 186 us -> 121 us (0.65)
  Pallas kernels: 185 us -> 120 us
    pallas_call x1, Pallas kernels: 58.6 us -> 2.67 us  [per_device(): pl.pallas_call(leave, name='leave', out_shape=(jax.ShapeDtypeStruct((toke...]
    pallas_call x1, Pallas kernels: 127 us -> 118 us  [per_device(): pl.pallas_call(kernel, name='semi_nmf', out_shape=(jax.ShapeDtypeStruct((...]
where the time goes in v3:
time: 121 us
  Pallas kernels  120 us (99%)
    pallas_call x1, Pallas kernels, per_device(): pl.pallas_call(kernel, name='semi_nmf', out_shape=(jax.ShapeDtypeStruct((...  118 us
    pallas_call x1, Pallas kernels, per_device(): pl.pallas_call(leave, name='leave', out_shape=(jax.ShapeDtypeStruct((toke...  2.67 us

profile of v3, /device:TPU:1, one launch (start us, length us, event | category | flops | bytes accessed | tf_op | source)
XLA Modules:
  0.0 120.9 jit_solution(11177106165483318340)
XLA Ops:
  0.6 117.6 %semi_nmf.1 = (f32[256,512]{1,0:T(8,128)}, f32[1792,256]{1,0:T(8,128)}) custom-call(bf16[512,1792]{1,0:T(8,128)(2,1)} %acts.1, f32[1792,256]{1,0:T(8,128)} %dic.1, f32[512,256]{1,0:T(8,128)} %codes.1), custom_call_target="tpu_custom_call" | custom-call | tf_op jit(solution)/shard_map/semi_nmf/pallas_call | solution.py:314
  118.2 2.7 %leave.1 = (f32[512,256]{1,0:T(8,128)}, f32[1792,256]{1,0:T(8,128)}) custom-call(f32[256,512]{1,0:T(8,128)} %get-tuple-element.4.out_t, f32[1792,256]{1,0:T(8,128)} %get-tuple-element.5.dict_in), custom_call_target="tpu_custom_call" | custom-call | tf_op jit(solution)/shard_map/leave/pallas_call | solution.py:336

commit v4 on v3

--- a/solution.py
+++ b/solution.py
@@ -72,22 +72,26 @@
     lax.fori_loop(first, last, body, 0)
 
 
-def update(part, proj, gram, codes):
+def gram_products(gram, codes):
     both = jnp.concatenate([jnp.maximum(-gram, 0.0), jnp.maximum(gram, 0.0)], axis=0)
-    prod = jnp.dot(both, codes, precision=HIGHEST, preferred_element_type=jnp.float32)
-    n = gram.shape[0]
-    numer = jnp.maximum(proj, 0.0) + prod[:n]
-    denom = jnp.maximum(jnp.maximum(-proj, 0.0) + prod[n:], floor_value)
+    return jnp.dot(both, codes, precision=HIGHEST, preferred_element_type=jnp.float32)
+
+
+def update(part, proj, prod, p):
+    n = prod.shape[0] // 2
+    numer = jnp.maximum(proj, 0.0) + prod[p * 8 : p * 8 + 8]
+    denom = jnp.maximum(jnp.maximum(-proj, 0.0) + prod[n + p * 8 : n + p * 8 + 8], floor_value)
     return part * jnp.sqrt(numer / denom)
 
 
 def kernel(
     acts, dic, codes, out_t, dict_out,
-    dt, ct, proj, gram, proj_in, gram_in, gram_tiles, mid,
+    dt, ct, proj, gram, gram_in, gram_tiles, mid,
     gk, gk_c, gk_x, gk_y, gk_z, ginv,
     cr, cr_c, cr_x0, cr_s0, cr_y0, cr_y1, cr_s1, cr_x1, full,
-    proj2, gram2, proj2_in, gram2_in, gram2_tiles,
-    zs, zr, ys, yr, xs, xr, cs, crs,
+    proj2, gram2, gram2_in, gram2_tiles,
+    a1, a2, a3, a4, a5, b1, b2, b3, b4, b5,
+    zs, zr, ds, dr, ys, yr, xs, xr, cs, crs,
 ):
     tok, z = lax.axis_index("tok"), lax.axis_index("hid")
     core, x, y = lax.rem(tok, 2), lax.rem(tok // 2, XS), tok // (2 * XS)
@@ -98,6 +102,8 @@
 
     zorder = (4, 3, 5, 2, 6, 1, 7)
     xorder = (2, 1, 3)
+
+    bufs, bufs2 = (a1, a2, a3, a4, a5), (b1, b2, b3, b4, b5)
 
     barrier = pltpu.get_barrier_semaphore()
     partners = [at(dz=o) for o in zorder] + [at(dy=o) for o in zorder] + [at(dx=o) for o in xorder] + [at(dc=1)]
@@ -116,16 +122,77 @@
 
     n = COMP // ZS
 
-    def scatter_z(part, slots, sem):
-        out = []
-        for o in zorder:
-            dev = at(dz=o)
-            out.append(push(part.at[rows(dev[1], n)], slots.at[o - 1], zs.at[sem, o - 1], zr.at[sem, o - 1], dev))
-        return out
-
-    def gather_z(buf, sem):
-        own = buf.at[rows(z, n)]
-        return [push(own, own, zs.at[sem, o - 1], zr.at[sem, o - 1], at(dz=o)) for o in zorder]
+    pieces = n // 8
+    ways = (1, -1)
+
+    def chunk(owner, p, size=1):
+        return pl.ds(pl.multiple_of(owner * n + p * 8, 8), size * 8)
+
+    def scatter_z(part, bufs, phase):
+        via1, via2, relay, fin1, fin2 = bufs
+        held = {}
+        for i, d in enumerate(ways):
+            for p in range(pieces // 2):
+                src = part.at[chunk(lax.rem(z + 4, ZS), p + i * (pieces // 2))]
+                ss, rs = zs.at[phase, i, p], zr.at[phase, i, p]
+                held["via2", i, p + i * (pieces // 2)] = push(src, via2.at[i, pl.ds(p * 8, 8)], ss, rs, at(dz=2 * d + ZS))
+        for p in range(pieces):
+            for i, d in enumerate(ways):
+                src = part.at[chunk(lax.rem(z + 3 * d + ZS, ZS), p)]
+                ss, rs = zs.at[phase, i, 2 + p], zr.at[phase, i, 2 + p]
+                held["via1", i, p] = push(src, via1.at[i, pl.ds(p * 8, 8)], ss, rs, at(dz=d + ZS))
+        for i, d in enumerate(ways):
+            src = part.at[chunk(lax.rem(z + d + ZS, ZS), 0, pieces)]
+            held["fin1", i] = push(src, fin1.at[i], zs.at[phase, i, 6], zr.at[phase, i, 6], at(dz=d + ZS))
+        return held
+
+    def relay_z(part, bufs, phase, held):
+        via1, via2, relay, fin1, fin2 = bufs
+        for p in range(pieces):
+            for i, d in enumerate(ways):
+                span = pl.ds(p * 8, 8)
+                held["via1", i, p].wait_recv()
+                total = part[chunk(lax.rem(z + 2 * d + ZS, ZS), p), :] + via1[i, span, :]
+                if p // (pieces // 2) == i:
+                    held["via2", i, p].wait_recv()
+                    total += via2[i, pl.ds((p - i * (pieces // 2)) * 8, 8), :]
+                relay[i, span, :] = total
+                ss, rs = zs.at[phase, i, 7 + p], zr.at[phase, i, 7 + p]
+                held["fin2", i, p] = push(relay.at[i, span], fin2.at[i, span], ss, rs, at(dz=2 * d + ZS))
+
+    def summed_z(part, bufs, held, p):
+        via1, via2, relay, fin1, fin2 = bufs
+        span = pl.ds(p * 8, 8)
+        total = part[chunk(z, p), :]
+        for i in range(2):
+            if p == 0:
+                held["fin1", i].wait_recv()
+            total += fin1[i, span, :]
+        for i in range(2):
+            held["fin2", i, p].wait_recv()
+            total += fin2[i, span, :]
+        return total
+
+    def gather_z(buf, phase, held, p):
+        spot = buf.at[chunk(z, p)]
+        for j, hops in ((0, 2), (4, 1)):
+            for i, d in enumerate(ways):
+                dev = at(dz=hops * d + ZS)
+                held[hops, i, p] = push(spot, spot, zs.at[phase, i, j + p], zr.at[phase, i, j + p], dev)
+
+    def forward_z(buf, phase, held):
+        for p in range(pieces):
+            for i, d in enumerate(ways):
+                held[2, i, p].wait_recv()
+                spot = buf.at[chunk(lax.rem(z - 2 * d + ZS, ZS), p)]
+                if p // (pieces // 2) == i:
+                    q = 8 + p - i * (pieces // 2)
+                    held[4, i, p] = push(spot, spot, zs.at[phase, i, q], zr.at[phase, i, q], at(dz=2 * d + ZS))
+                held[3, i, p] = push(spot, spot, zs.at[phase, i, 10 + p], zr.at[phase, i, 10 + p], at(dz=d + ZS))
+        for key, c in held.items():
+            c.wait_send()
+            if key[0] != 2:
+                c.wait_recv()
 
     def send_gram(matrix, part, slots, sem):
         picked = [matrix[pl.ds(pl.multiple_of(j * n + x * 8, 8), 8), :] for j in range(ZS)]
@@ -136,14 +203,17 @@
         out = []
         for o in zorder:
             dev = at(dz=o)
-            out.append(push(part.at[dev[1]], slots.at[o - 1], zs.at[sem, o - 1], zr.at[sem, o - 1], dev))
+            out.append(push(part.at[dev[1]], slots.at[o - 1], ds.at[sem, o - 1], dr.at[sem, o - 1], dev))
         return out
 
     def share_gram(sent, part, slots, tiles, step):
         finish(sent)
         spot = tiles.at[core, x]
         spot[...] = part[z] + sum(slots[i] for i in range(ZS - 1))
-        finish([push(spot, spot, xs.at[step, o - 1], xr.at[step, o - 1], at(dx=o)) for o in xorder])
+        return [push(spot, spot, xs.at[step, o - 1], xr.at[step, o - 1], at(dx=o)) for o in xorder]
+
+    def whole_gram(sent, tiles, step):
+        finish(sent)
         spot = tiles.at[core]
         push(spot, spot, cs.at[step], crs.at[step], at(dc=1)).wait()
         return jnp.concatenate([tiles[i].reshape(n, 128) for i in range(2)], axis=1)
@@ -155,15 +225,20 @@
     dt[...] = dic[...].T
     proj[...] = lax.dot_general(dt[...].astype(jnp.bfloat16), acts[...], NT, preferred_element_type=jnp.float32)
     pl.semaphore_wait(barrier, len(partners))
-    sent_gram = send_gram(dt, gram, gram_in, 1)
-    sent = scatter_z(proj, proj_in, 0)
+    sent_gram = send_gram(dt, gram, gram_in, 0)
+    held = scatter_z(proj, bufs, 0)
     ct[...] = codes[...].T
     own = rows(z, n)
-    gram_sum = share_gram(sent_gram, gram, gram_in, gram_tiles, 4)
-    finish(sent)
-    proj_sum = proj[own, :] + sum(proj_in[i] for i in range(ZS - 1))
-    mid[own, :] = update(ct[own, :], proj_sum, gram_sum, ct[...])
-    finish(gather_z(mid, 2))
+    sent_gram = share_gram(sent_gram, gram, gram_in, gram_tiles, 4)
+    relay_z(proj, bufs, 0, held)
+    prod = gram_products(whole_gram(sent_gram, gram_tiles, 4), ct[...])
+    passed = {}
+    for p in range(pieces):
+        mid[chunk(z, p), :] = update(ct[chunk(z, p), :], summed_z(proj, bufs, held, p), prod, p)
+        gather_z(mid, 1, passed, p)
+    for c in held.values():
+        c.wait_send()
+    forward_z(mid, 1, passed)
 
     low = mid[...].astype(jnp.bfloat16)
     low_own = mid[own, :].astype(jnp.bfloat16)
@@ -213,7 +288,7 @@
     finish(g_y)
     spot = gk_z.at[z, core]
     spot[...] = sum(gk_y[i] for i in range(YS))
-    g_z = [push(spot, spot, zs.at[6, o - 1], zr.at[6, o - 1], at(dz=o)) for o in zorder]
+    g_z = [push(spot, spot, ds.at[2, o - 1], dr.at[2, o - 1], at(dz=o)) for o in zorder]
     finish(c0)
     cr_s0[...] = cr_c[rows(x, xspan), :] + cr_x0[0] + cr_x0[1] + cr_x0[2]
     c0 = []
@@ -268,15 +343,20 @@
     solve(part0, halftiles)
     c0.wait()
     solve(0, part0)
-    sent_gram = send_gram(dt, gram2, gram2_in, 4)
+    sent_gram = send_gram(dt, gram2, gram2_in, 1)
     proj2[...] = lax.dot_general(dt[...].astype(jnp.bfloat16), acts[...], NT, preferred_element_type=jnp.float32)
-    sent = scatter_z(proj2, proj2_in, 3)
+    held = scatter_z(proj2, bufs2, 2)
     dict_out[...] = dt[...].T
-    gram_sum = share_gram(sent_gram, gram2, gram2_in, gram2_tiles, 5)
-    finish(sent)
-    proj_sum = proj2[own, :] + sum(proj2_in[i] for i in range(ZS - 1))
-    out_t[own, :] = update(mid[own, :], proj_sum, gram_sum, mid[...])
-    finish(gather_z(out_t, 5))
+    sent_gram = share_gram(sent_gram, gram2, gram2_in, gram2_tiles, 5)
+    relay_z(proj2, bufs2, 2, held)
+    prod = gram_products(whole_gram(sent_gram, gram2_tiles, 5), mid[...])
+    passed = {}
+    for p in range(pieces):
+        out_t[chunk(z, p), :] = update(mid[chunk(z, p), :], summed_z(proj2, bufs2, held, p), prod, p)
+        gather_z(out_t, 3, passed, p)
+    for c in held.values():
+        c.wait_send()
+    forward_z(out_t, 3, passed)
 
 
 def leave(out_t, dict_in, codes_out, dict_out, held_t, held_codes, held_dict, ins, outs):
@@ -309,6 +389,7 @@
     half = hid * COMP // 2 // 128
     cut = (hid // 256 - hid // 256 // 3) * COMP
     rest = half - cut
+    sums = (v(2, n, tokens), v(2, n // 2, tokens), v(2, n, tokens), v(2, n, tokens), v(2, n, tokens))
     vmem = pl.BlockSpec(memory_space=pltpu.VMEM)
     dma = pltpu.SemaphoreType.DMA
     out_t, dict_new = pl.pallas_call(
@@ -319,13 +400,14 @@
         out_specs=(vmem, vmem),
         scratch_shapes=[
             v(COMP, hid), v(COMP, tokens), v(COMP, tokens), v(ZS, 8, 128),
-            v(ZS - 1, n, tokens), v(ZS - 1, 8, 128), v(2, XS, 8, 128), v(COMP, tokens),
+            v(ZS - 1, 8, 128), v(2, XS, 8, 128), v(COMP, tokens),
             v(2, n // 2, COMP), v(n // 2, COMP), v(XS, n // 2, COMP), v(YS, n // 2, COMP), v(ZS, 2, n // 2, COMP),
             v(COMP, COMP),
             v(2, half, 128), v(half, 128), v(XS - 1, cut // XS, 128), v(cut // XS, 128), v(YS - 1, cut // XS // YS, 128),
             v(YS - 1, rest // YS, 128), v(rest // YS, 128), v(XS - 1, rest // YS // XS, 128), v(2, half, 128),
-            v(COMP, tokens), v(ZS, 8, 128), v(ZS - 1, n, tokens), v(ZS - 1, 8, 128), v(2, XS, 8, 128),
-            dma((7, ZS - 1)), dma((7, ZS - 1)), dma((5, YS - 1)), dma((5, YS - 1)),
+            v(COMP, tokens), v(ZS, 8, 128), v(ZS - 1, 8, 128), v(2, XS, 8, 128),
+            *sums, *sums,
+            dma((4, 2, 14)), dma((4, 2, 14)), dma((3, ZS - 1)), dma((3, ZS - 1)), dma((5, YS - 1)), dma((5, YS - 1)),
             dma((7, XS - 1)), dma((7, XS - 1)), dma((8,)), dma((8,)),
         ],
         compiler_params=pltpu.CompilerParams(

time: 121 us -> 107 us (0.88)
  Pallas kernels: 120 us -> 106 us
    pallas_call x1, Pallas kernels: 118 us -> 103 us  [per_device(): pl.pallas_call(kernel, name='semi_nmf', out_shape=(jax.ShapeDtypeStruct((...]
where the time goes in v4:
time: 107 us
  Pallas kernels  106 us (99%)
    pallas_call x1, Pallas kernels, per_device(): pl.pallas_call(kernel, name='semi_nmf', out_shape=(jax.ShapeDtypeStruct((...  103 us
    pallas_call x1, Pallas kernels, per_device(): pl.pallas_call(leave, name='leave', out_shape=(jax.ShapeDtypeStruct((toke...  2.67 us

profile of v4, /device:TPU:1, one launch (start us, length us, event | category | flops | bytes accessed | tf_op | source)
XLA Modules:
  0.0 106.6 jit_solution(18285964422206350067)
XLA Ops:
  0.6 103.3 %semi_nmf.1 = (f32[256,512]{1,0:T(8,128)}, f32[1792,256]{1,0:T(8,128)}) custom-call(bf16[512,1792]{1,0:T(8,128)(2,1)} %acts.1, f32[1792,256]{1,0:T(8,128)} %dic.1, f32[512,256]{1,0:T(8,128)} %codes.1), custom_call_target="tpu_custom_call" | custom-call | tf_op jit(solution)/shard_map/semi_nmf/pallas_call | solution.py:395
  103.9 2.7 %leave.1 = (f32[512,256]{1,0:T(8,128)}, f32[1792,256]{1,0:T(8,128)}) custom-call(f32[256,512]{1,0:T(8,128)} %get-tuple-element.4.out_t, f32[1792,256]{1,0:T(8,128)} %get-tuple-element.5.dict_in), custom_call_target="tpu_custom_call" | custom-call | tf_op jit(solution)/shard_map/leave/pallas_call | solution.py:418

commit v5 on v4

--- a/solution.py
+++ b/solution.py
@@ -42,16 +42,13 @@
     lane = lax.broadcasted_iota(jnp.int32, (BLOCK, size), 1) - k * BLOCK
     wide_row = lax.broadcasted_iota(jnp.int32, (BLOCK, size), 0)
     for i in range(BLOCK):
-        inv = 1.0 / cols[i][i : i + 1, :]
-        scaled = cols[i] * inv
-        scaled2 = jnp.concatenate([scaled, scaled], axis=1)
-        inv2 = jnp.concatenate([inv, inv], axis=1)
+        scaled = jnp.where(row == i, -1.0, cols[i]) * (1.0 / cols[i][i : i + 1, :])
+        wide = jnp.concatenate([scaled] * (size // 128), axis=1)
         pivot = panel[i : i + 1, :]
-        new = jnp.where(wide_row == i, pivot * inv2, panel - scaled2 * pivot)
-        panel = jnp.where(lane == i, jnp.where(wide_row == i, inv2, -scaled2), new)
+        panel = jnp.where(lane == i, -wide, jnp.where(wide_row == i, 0.0, panel) - wide * pivot)
         for j in range(i + 1, BLOCK):
             c = cols[j][i : i + 1, :]
-            cols[j] = jnp.where(row == i, c * inv, cols[j] - scaled * c)
+            cols[j] = jnp.where(row == i, 0.0, cols[j]) - scaled * c
     return panel
 
 
@@ -84,14 +81,16 @@
     return part * jnp.sqrt(numer / denom)
 
 
+def part_list(halftiles):
+    b, c = halftiles - 2 * (halftiles * 2 // 7), halftiles * 2 // 7
+    return ((0, b, "xy"), (b, c, "xy"), (b + c, c, "yx"))
+
+
 def kernel(
-    acts, dic, codes, out_t, dict_out,
-    dt, ct, proj, gram, gram_in, gram_tiles, mid,
+    acts_in, dic_in, codes_in, out_t, dict_out,
+    acts, dic, codes, loaded, dt, ct, proj, gram, gram_in, gram_tiles, mid,
     gk, gk_c, gk_x, gk_y, gk_z, ginv,
-    cr, cr_c, cr_x0, cr_s0, cr_y0, cr_y1, cr_s1, cr_x1, full,
-    proj2, gram2, gram2_in, gram2_tiles,
-    a1, a2, a3, a4, a5, b1, b2, b3, b4, b5,
-    zs, zr, ds, dr, ys, yr, xs, xr, cs, crs,
+    cr, cr_c, full, *rest,
 ):
     tok, z = lax.axis_index("tok"), lax.axis_index("hid")
     core, x, y = lax.rem(tok, 2), lax.rem(tok // 2, XS), tok // (2 * XS)
@@ -103,7 +102,10 @@
     zorder = (4, 3, 5, 2, 6, 1, 7)
     xorder = (2, 1, 3)
 
-    bufs, bufs2 = (a1, a2, a3, a4, a5), (b1, b2, b3, b4, b5)
+    in1, sum1, in2, rest = rest[:3], rest[3:6], rest[6:9], rest[9:]
+    (proj2, gram2, gram2_in, gram2_tiles), rest = rest[:4], rest[4:]
+    bufs, bufs2, rest = rest[:5], rest[5:10], rest[10:]
+    zs, zr, ds, dr, ys, yr, xs, xr, cs, crs = rest
 
     barrier = pltpu.get_barrier_semaphore()
     partners = [at(dz=o) for o in zorder] + [at(dy=o) for o in zorder] + [at(dx=o) for o in xorder] + [at(dc=1)]
@@ -206,13 +208,13 @@
             out.append(push(part.at[dev[1]], slots.at[o - 1], ds.at[sem, o - 1], dr.at[sem, o - 1], dev))
         return out
 
-    def share_gram(sent, part, slots, tiles, step):
+    def share_gram(sent, part, slots, tiles, step, _):
         finish(sent)
         spot = tiles.at[core, x]
         spot[...] = part[z] + sum(slots[i] for i in range(ZS - 1))
         return [push(spot, spot, xs.at[step, o - 1], xr.at[step, o - 1], at(dx=o)) for o in xorder]
 
-    def whole_gram(sent, tiles, step):
+    def whole_gram(sent, tiles, _, step):
         finish(sent)
         spot = tiles.at[core]
         push(spot, spot, cs.at[step], crs.at[step], at(dc=1)).wait()
@@ -222,16 +224,25 @@
         for c in copies:
             c.wait()
 
+    loads = [
+        pltpu.make_async_copy(src, dst, loaded.at[i])
+        for i, (src, dst) in enumerate(((dic_in, dic), (acts_in, acts), (codes_in, codes)))
+    ]
+    for c in loads:
+        c.start()
+    loads[0].wait()
     dt[...] = dic[...].T
+    loads[1].wait()
     proj[...] = lax.dot_general(dt[...].astype(jnp.bfloat16), acts[...], NT, preferred_element_type=jnp.float32)
     pl.semaphore_wait(barrier, len(partners))
     sent_gram = send_gram(dt, gram, gram_in, 0)
     held = scatter_z(proj, bufs, 0)
+    loads[2].wait()
     ct[...] = codes[...].T
     own = rows(z, n)
-    sent_gram = share_gram(sent_gram, gram, gram_in, gram_tiles, 4)
+    sent_gram = share_gram(sent_gram, gram, gram_in, gram_tiles, 7, 8)
     relay_z(proj, bufs, 0, held)
-    prod = gram_products(whole_gram(sent_gram, gram_tiles, 4), ct[...])
+    prod = gram_products(whole_gram(sent_gram, gram_tiles, 7, 8), ct[...])
     passed = {}
     for p in range(pieces):
         mid[chunk(z, p), :] = update(ct[chunk(z, p), :], summed_z(proj, bufs, held, p), prod, p)
@@ -243,93 +254,115 @@
     low = mid[...].astype(jnp.bfloat16)
     low_own = mid[own, :].astype(jnp.bfloat16)
     gk[...] = lax.dot_general(low_own, low, NT, preferred_element_type=jnp.float32).reshape(gk.shape)
-    g_c = push(gk.at[1 - core], gk_c, cs.at[0], crs.at[0], at(dc=1))
+    g_c = push(gk.at[1 - core], gk_c, cs.at[6], crs.at[6], at(dc=1))
 
     halftiles = acts.shape[1] // 256
-    part0 = halftiles - halftiles // 3
-    cut = part0 * COMP
-    rest = halftiles * COMP - cut
-
-    def cross(which, first, last):
-        for j in range(first, last):
-            lanes = pl.ds(pl.multiple_of((which * halftiles + j) * 128, 128), 128)
-            cr[which, pl.ds(j * COMP, COMP), :] = jnp.dot(low, acts[:, lanes], preferred_element_type=jnp.float32)
-
-    head, tail = pl.ds(0, cut), pl.ds(cut, rest)
-    cross(1 - core, 0, part0)
-    c_c0 = push(cr.at[1 - core, head], cr_c.at[head], cs.at[1], crs.at[1], at(dc=1))
-    cross(1 - core, part0, halftiles)
-    c_c1 = push(cr.at[1 - core, tail], cr_c.at[tail], cs.at[2], crs.at[2], at(dc=1))
+    parts = part_list(halftiles)
+
+    def cross(which, p):
+        first, count, _ = parts[p]
+        lanes = pl.ds(pl.multiple_of((which * halftiles + first) * 128, 128), count * 128)
+        block = jnp.dot(low, acts[:, lanes], preferred_element_type=jnp.float32)
+        for j in range(count):
+            cr[which, pl.ds((first + j) * COMP, COMP), :] = block[:, j * 128 : j * 128 + 128]
+
+    axes = {"x": (x, XS, xorder, xs, xr), "y": (y, YS, zorder, ys, yr)}
+
+    def shares(p):
+        first, count, order = parts[p]
+        one, two = axes[order[0]], axes[order[1]]
+        size = count * COMP
+        return first * COMP, size, one, two, size // one[1], size // one[1] // two[1]
+
+    def span_of(base, i, size):
+        return pl.ds(pl.multiple_of(base + i * size, size), size)
+
+    def along(name, row, src_of, dst_of):
+        me, count, order, ss, rs = axes[name]
+        out = []
+        for o in order:
+            dev = at(dx=o) if name == "x" else at(dy=o)
+            out.append(push(src_of(lax.rem(me + o, count)), dst_of(o), ss.at[row, o - 1], rs.at[row, o - 1], dev))
+        return out
+
+    def send_core(p):
+        base, size, _, _, _, _ = shares(p)
+        span = pl.ds(base, size)
+        return [push(cr.at[1 - core, span], cr_c.at[span], cs.at[p], crs.at[p], at(dc=1))]
+
+    def send_first(p, copies):
+        finish(copies)
+        base, size, one, two, n1, n2 = shares(p)
+        span = pl.ds(base, size)
+        cr_c[span, :] += cr[core, span, :]
+        return along(parts[p][2][0], 2 * p, lambda i: cr_c.at[span_of(base, i, n1)], lambda o: in1[p].at[o - 1])
+
+    def send_second(p, copies):
+        finish(copies)
+        base, size, one, two, n1, n2 = shares(p)
+        sum1[p][...] = cr_c[span_of(base, one[0], n1), :] + sum(in1[p][i] for i in range(one[1] - 1))
+        return along(parts[p][2][1], 2 * p, lambda i: sum1[p].at[span_of(0, i, n2)], lambda o: in2[p].at[o - 1])
+
+    def gather_second(p, copies):
+        finish(copies)
+        base, size, one, two, n1, n2 = shares(p)
+        spot = full.at[core, span_of(base, one[0] * two[1] + two[0], n2)]
+        spot[...] = sum1[p][span_of(0, two[0], n2), :] + sum(in2[p][i] for i in range(two[1] - 1))
+        return along(parts[p][2][1], 2 * p + 1, lambda i: spot, lambda o: spot)
+
+    def gather_first(p, copies):
+        finish(copies)
+        base, size, one, two, n1, n2 = shares(p)
+        spot = full.at[core, span_of(base, one[0], n1)]
+        return along(parts[p][2][0], 2 * p + 1, lambda i: spot, lambda o: spot)
+
+    def gather_core(p, copies):
+        finish(copies)
+        base, size, _, _, _, _ = shares(p)
+        spot = full.at[core, pl.ds(base, size)]
+        return [push(spot, spot, cs.at[3 + p], crs.at[3 + p], at(dc=1))]
+
+    c = [None] * 3
+    for p in range(3):
+        cross(1 - core, p)
+        c[p] = send_core(p)
     g_c.wait()
     gk_x[x] = gk[core] + gk_c[...]
-    g_x = [push(gk_x.at[x], gk_x.at[x], xs.at[0, o - 1], xr.at[0, o - 1], at(dx=o)) for o in xorder]
-    cross(core, 0, halftiles)
-    c_c0.wait()
-    cr_c[head, :] += cr[core, head, :]
-    xspan, xpiece = cut // XS, cut // XS // YS
-    yspan, ypiece = rest // YS, rest // YS // XS
-
-    def tail_rows(i, size):
-        return pl.ds(pl.multiple_of(cut + i * size, size), size)
-
-    c0 = []
-    for o in xorder:
-        px = lax.rem(x + o, XS)
-        c0.append(push(cr_c.at[rows(px, xspan)], cr_x0.at[o - 1], xs.at[1, o - 1], xr.at[1, o - 1], at(dx=o)))
+    g_x = along("x", 6, lambda i: gk_x.at[x], lambda o: gk_x.at[x])
+    for p in range(3):
+        cross(core, p)
+    c[0] = send_first(0, c[0])
+    c[1] = send_first(1, c[1])
     finish(g_x)
     gk_y[y] = sum(gk_x[i] for i in range(XS))
-    g_y = [push(gk_y.at[y], gk_y.at[y], ys.at[0, o - 1], yr.at[0, o - 1], at(dy=o)) for o in zorder]
-    c_c1.wait()
-    cr_c[tail, :] += cr[core, tail, :]
-    c1 = []
-    for o in zorder:
-        py = lax.rem(y + o, YS)
-        c1.append(push(cr_c.at[tail_rows(py, yspan)], cr_y1.at[o - 1], ys.at[1, o - 1], yr.at[1, o - 1], at(dy=o)))
+    g_y = along("y", 6, lambda i: gk_y.at[y], lambda o: gk_y.at[y])
+    c[2] = send_first(2, c[2])
+    c[0] = send_second(0, c[0])
+    c[1] = send_second(1, c[1])
     finish(g_y)
     spot = gk_z.at[z, core]
     spot[...] = sum(gk_y[i] for i in range(YS))
     g_z = [push(spot, spot, ds.at[2, o - 1], dr.at[2, o - 1], at(dz=o)) for o in zorder]
-    finish(c0)
-    cr_s0[...] = cr_c[rows(x, xspan), :] + cr_x0[0] + cr_x0[1] + cr_x0[2]
-    c0 = []
-    for o in zorder:
-        py = lax.rem(y + o, YS)
-        c0.append(push(cr_s0.at[rows(py, xpiece)], cr_y0.at[o - 1], ys.at[2, o - 1], yr.at[2, o - 1], at(dy=o)))
-    finish(c1)
-    cr_s1[...] = cr_c[tail_rows(y, yspan), :] + sum(cr_y1[i] for i in range(YS - 1))
-    c1 = []
-    for o in xorder:
-        px = lax.rem(x + o, XS)
-        c1.append(push(cr_s1.at[rows(px, ypiece)], cr_x1.at[o - 1], xs.at[2, o - 1], xr.at[2, o - 1], at(dx=o)))
-    finish(c1)
-    spot = full.at[core, tail_rows(y * XS + x, ypiece)]
-    spot[...] = cr_s1[rows(x, ypiece), :] + cr_x1[0] + cr_x1[1] + cr_x1[2]
-    c1 = [push(spot, spot, xs.at[3, o - 1], xr.at[3, o - 1], at(dx=o)) for o in xorder]
+    c[2] = send_second(2, c[2])
+    c[0] = gather_second(0, c[0])
+    c[1] = gather_second(1, c[1])
+    c[2] = gather_second(2, c[2])
     finish(g_z)
     spot = gk_z.at[:, core]
-    g_c = push(spot, spot, cs.at[3], crs.at[3], at(dc=1))
-    finish(c0)
-    spot = full.at[core, rows(x * YS + y, xpiece)]
-    spot[...] = cr_s0[rows(y, xpiece), :] + sum(cr_y0[i] for i in range(YS - 1))
-    c0 = [push(spot, spot, ys.at[3, o - 1], yr.at[3, o - 1], at(dy=o)) for o in zorder]
-    finish(c1)
-    spot = full.at[core, tail_rows(y, yspan)]
-    c1 = [push(spot, spot, ys.at[4, o - 1], yr.at[4, o - 1], at(dy=o)) for o in zorder]
+    g_c = push(spot, spot, cs.at[7], crs.at[7], at(dc=1))
+    c[2] = gather_first(2, c[2])
     g_c.wait()
     ginv[...] = gk_z[...].reshape(COMP, COMP)
 
-    steps = COMP // BLOCK
-    invert_blocks(ginv, 0, steps // 2)
-    finish(c0)
-    spot = full.at[core, rows(x, xspan)]
-    c0 = [push(spot, spot, xs.at[6, o - 1], xr.at[6, o - 1], at(dx=o)) for o in xorder]
-    finish(c1)
-    spot = full.at[core, tail]
-    c1 = push(spot, spot, cs.at[6], crs.at[6], at(dc=1))
-    invert_blocks(ginv, steps // 2, steps)
-    finish(c0)
-    spot = full.at[core, head]
-    c0 = push(spot, spot, cs.at[7], crs.at[7], at(dc=1))
+    invert_blocks(ginv, 0, 2)
+    c[0] = gather_first(0, c[0])
+    c[1] = gather_first(1, c[1])
+    invert_blocks(ginv, 2, 8)
+    c[0] = gather_core(0, c[0])
+    c[2] = gather_core(2, c[2])
+    invert_blocks(ginv, 8, 12)
+    c[1] = gather_core(1, c[1])
+    invert_blocks(ginv, 12, 16)
 
     def solve(first, last):
         for j in range(first, last):
@@ -339,17 +372,16 @@
             for i in range(2):
                 dt[:, (i * halftiles + j) * 128 : (i * halftiles + j + 1) * 128] = solved[:, i * 128 : i * 128 + 128]
 
-    c1.wait()
-    solve(part0, halftiles)
-    c0.wait()
-    solve(0, part0)
+    for p in (0, 2, 1):
+        finish(c[p])
+        solve(parts[p][0], parts[p][0] + parts[p][1])
     sent_gram = send_gram(dt, gram2, gram2_in, 1)
     proj2[...] = lax.dot_general(dt[...].astype(jnp.bfloat16), acts[...], NT, preferred_element_type=jnp.float32)
     held = scatter_z(proj2, bufs2, 2)
     dict_out[...] = dt[...].T
-    sent_gram = share_gram(sent_gram, gram2, gram2_in, gram2_tiles, 5)
+    sent_gram = share_gram(sent_gram, gram2, gram2_in, gram2_tiles, 8, 9)
     relay_z(proj2, bufs2, 2, held)
-    prod = gram_products(whole_gram(sent_gram, gram2_tiles, 5), mid[...])
+    prod = gram_products(whole_gram(sent_gram, gram2_tiles, 8, 9), mid[...])
     passed = {}
     for p in range(pieces):
         out_t[chunk(z, p), :] = update(mid[chunk(z, p), :], summed_z(proj2, bufs2, held, p), prod, p)
@@ -359,25 +391,17 @@
     forward_z(out_t, 3, passed)
 
 
-def leave(out_t, dict_in, codes_out, dict_out, held_t, held_codes, held_dict, ins, outs):
+def leave(out_t, dict_in, codes_out, dict_out, held, sem):
     parts = 4
     step = dict_in.shape[0] // parts
     spots = [pl.ds(i * step, step) for i in range(parts)]
-    first = pltpu.make_async_copy(out_t, held_t, ins.at[parts])
-    first.start()
-    arriving = [pltpu.make_async_copy(dict_in.at[p], held_dict.at[p], ins.at[i]) for i, p in enumerate(spots)]
-    for c in arriving:
+    copies = [pltpu.make_async_copy(dict_in.at[p], dict_out.at[p], sem.at[i]) for i, p in enumerate(spots)]
+    for c in copies:
         c.start()
-    leaving = []
-    for i, p in enumerate(spots):
-        arriving[i].wait()
-        leaving.append(pltpu.make_async_copy(held_dict.at[p], dict_out.at[p], outs.at[i]))
-        leaving[-1].start()
-    first.wait()
-    held_codes[...] = held_t[...].T
-    leaving.append(pltpu.make_async_copy(held_codes, codes_out, outs.at[parts]))
-    leaving[-1].start()
-    for c in leaving:
+    held[...] = out_t[...].T
+    copies.append(pltpu.make_async_copy(held, codes_out, sem.at[parts]))
+    copies[-1].start()
+    for c in copies:
         c.wait()
 
 
@@ -387,42 +411,45 @@
     v = lambda *s: pltpu.VMEM(s, f32)
     n = COMP // ZS
     half = hid * COMP // 2 // 128
-    cut = (hid // 256 - hid // 256 // 3) * COMP
-    rest = half - cut
+    count = {"x": XS, "y": YS}
+    shapes = [(k * COMP, count[order[0]], count[order[1]]) for _, k, order in part_list(hid // 256)]
     sums = (v(2, n, tokens), v(2, n // 2, tokens), v(2, n, tokens), v(2, n, tokens), v(2, n, tokens))
     vmem = pl.BlockSpec(memory_space=pltpu.VMEM)
+    anywhere = pl.BlockSpec(memory_space=pl.ANY)
     dma = pltpu.SemaphoreType.DMA
     out_t, dict_new = pl.pallas_call(
         kernel,
         name="semi_nmf",
-        out_shape=(jax.ShapeDtypeStruct((COMP, tokens), f32), jax.ShapeDtypeStruct((hid, COMP), f32)),
-        in_specs=[vmem] * 3,
+        out_shape=(pltpu.VMEM((COMP, tokens), f32), pltpu.VMEM((hid, COMP), f32)),
+        in_specs=[anywhere] * 3,
         out_specs=(vmem, vmem),
         scratch_shapes=[
+            pltpu.VMEM((tokens, hid), jnp.bfloat16), v(hid, COMP), v(tokens, COMP), dma((3,)),
             v(COMP, hid), v(COMP, tokens), v(COMP, tokens), v(ZS, 8, 128),
             v(ZS - 1, 8, 128), v(2, XS, 8, 128), v(COMP, tokens),
             v(2, n // 2, COMP), v(n // 2, COMP), v(XS, n // 2, COMP), v(YS, n // 2, COMP), v(ZS, 2, n // 2, COMP),
             v(COMP, COMP),
-            v(2, half, 128), v(half, 128), v(XS - 1, cut // XS, 128), v(cut // XS, 128), v(YS - 1, cut // XS // YS, 128),
-            v(YS - 1, rest // YS, 128), v(rest // YS, 128), v(XS - 1, rest // YS // XS, 128), v(2, half, 128),
+            v(2, half, 128), v(half, 128), v(2, half, 128),
+            *[v(one - 1, size // one, 128) for size, one, two in shapes],
+            *[v(size // one, 128) for size, one, two in shapes],
+            *[v(two - 1, size // one // two, 128) for size, one, two in shapes],
             v(COMP, tokens), v(ZS, 8, 128), v(ZS - 1, 8, 128), v(2, XS, 8, 128),
             *sums, *sums,
-            dma((4, 2, 14)), dma((4, 2, 14)), dma((3, ZS - 1)), dma((3, ZS - 1)), dma((5, YS - 1)), dma((5, YS - 1)),
-            dma((7, XS - 1)), dma((7, XS - 1)), dma((8,)), dma((8,)),
+            dma((4, 2, 14)), dma((4, 2, 14)), dma((3, ZS - 1)), dma((3, ZS - 1)), dma((7, YS - 1)), dma((7, YS - 1)),
+            dma((9, XS - 1)), dma((9, XS - 1)), dma((10,)), dma((10,)),
         ],
         compiler_params=pltpu.CompilerParams(
             collective_id=0, has_side_effects=True, vmem_limit_bytes=56 * 1024 * 1024
         ),
     )(acts, dictionary, codes)
-    anywhere = pl.BlockSpec(memory_space=pl.ANY)
     return pl.pallas_call(
         leave,
         name="leave",
         out_shape=(jax.ShapeDtypeStruct((tokens, COMP), f32), jax.ShapeDtypeStruct((hid, COMP), f32)),
-        in_specs=[anywhere] * 2,
+        in_specs=[vmem] * 2,
         out_specs=(anywhere, anywhere),
-        scratch_shapes=[v(COMP, tokens), v(tokens, COMP), v(hid, COMP), dma((5,)), dma((5,))],
-        compiler_params=pltpu.CompilerParams(vmem_limit_bytes=56 * 1024 * 1024),
+        scratch_shapes=[v(tokens, COMP), dma((5,))],
+        compiler_params=pltpu.CompilerParams(vmem_limit_bytes=16 * 1024 * 1024),
     )(out_t, dict_new)
 
 

time: 107 us -> 102 us (0.953)
  Pallas kernels: 106 us -> 101 us
    pallas_call x1, Pallas kernels: 103 us -> 100 us  [per_device(): pl.pallas_call(kernel, name='semi_nmf', out_shape=(pltpu.VMEM((COMP, toke...]
    pallas_call x1, Pallas kernels: 2.67 us -> 1.44 us  [per_device(): pl.pallas_call(leave, name='leave', out_shape=(jax.ShapeDtypeStruct((toke...]
where the time goes in v5:
time: 102 us
  Pallas kernels  101 us (99%)
    pallas_call x1, Pallas kernels, per_device(): pl.pallas_call(kernel, name='semi_nmf', out_shape=(pltpu.VMEM((COMP, toke...  100 us

profile of v5, /device:TPU:1, one launch (start us, length us, event | category | flops | bytes accessed | tf_op | source)
XLA Modules:
  0.0 102.1 jit_solution(18322715649816019992)
XLA Ops:
  0.6 100.0 %semi_nmf.1 = (f32[256,512]{1,0:T(8,128)S(1)}, f32[1792,256]{1,0:T(8,128)S(1)}) custom-call(bf16[512,1792]{1,0:T(8,128)(2,1)} %acts_in.1, f32[1792,256]{1,0:T(8,128)} %dic_in.1, f32[512,256]{1,0:T(8,128)} %codes_in.1), custom_call_target="tpu_custom_call" | custom-call | tf_op jit(solution)/shard_map/semi_nmf/pallas_call | solution.py:420
  100.6 1.4 %leave.1 = (f32[512,256]{1,0:T(8,128)}, f32[1792,256]{1,0:T(8,128)}) custom-call(f32[256,512]{1,0:T(8,128)S(1)} %get-tuple-element.4.out_t, f32[1792,256]{1,0:T(8,128)S(1)} %get-tuple-element.5.dict_in), custom_call_target="tpu_custom_call" | custom-call | tf_op jit(solution)/shard_map/leave/pallas_call | solution.py:445

commit v6 on v5

--- a/solution.py
+++ b/solution.py
@@ -23,6 +23,11 @@
     mid = rest.astype(jnp.bfloat16)
     low = (rest - mid.astype(jnp.float32)).astype(jnp.bfloat16)
     return hi, mid, low
+
+
+def split2(v):
+    hi = v.astype(jnp.bfloat16)
+    return jnp.concatenate([hi, (v - hi.astype(jnp.float32)).astype(jnp.bfloat16)], axis=0)
 
 
 def outer6(c, y):
@@ -198,10 +203,11 @@
 
     def send_gram(matrix, part, slots, sem):
         picked = [matrix[pl.ds(pl.multiple_of(j * n + x * 8, 8), 8), :] for j in range(ZS)]
-        part[...] = lax.dot_general(
-            jnp.concatenate(picked, axis=0), matrix[rows(core, 128), :], NT,
-            precision=HIGHEST, preferred_element_type=jnp.float32,
-        ).reshape(part.shape)
+        both = split2(jnp.concatenate(picked, axis=0))
+        prod = lax.dot_general(both, split2(matrix[rows(core, 128), :]), NT, preferred_element_type=jnp.float32)
+        m = 8 * ZS
+        tile = prod[:m, :128] + (prod[:m, 128:] + prod[m:, :128] + prod[m:, 128:])
+        part[...] = tile.reshape(part.shape)
         out = []
         for o in zorder:
             dev = at(dz=o)
@@ -343,26 +349,27 @@
     spot = gk_z.at[z, core]
     spot[...] = sum(gk_y[i] for i in range(YS))
     g_z = [push(spot, spot, ds.at[2, o - 1], dr.at[2, o - 1], at(dz=o)) for o in zorder]
+    c[0] = gather_second(0, c[0])
     c[2] = send_second(2, c[2])
-    c[0] = gather_second(0, c[0])
     c[1] = gather_second(1, c[1])
-    c[2] = gather_second(2, c[2])
     finish(g_z)
     spot = gk_z.at[:, core]
     g_c = push(spot, spot, cs.at[7], crs.at[7], at(dc=1))
-    c[2] = gather_first(2, c[2])
+    c[2] = gather_second(2, c[2])
     g_c.wait()
     ginv[...] = gk_z[...].reshape(COMP, COMP)
 
-    invert_blocks(ginv, 0, 2)
+    invert_blocks(ginv, 0, 3)
     c[0] = gather_first(0, c[0])
+    c[2] = gather_first(2, c[2])
+    invert_blocks(ginv, 3, 5)
     c[1] = gather_first(1, c[1])
-    invert_blocks(ginv, 2, 8)
+    invert_blocks(ginv, 5, 11)
     c[0] = gather_core(0, c[0])
+    invert_blocks(ginv, 11, 14)
+    c[1] = gather_core(1, c[1])
     c[2] = gather_core(2, c[2])
-    invert_blocks(ginv, 8, 12)
-    c[1] = gather_core(1, c[1])
-    invert_blocks(ginv, 12, 16)
+    invert_blocks(ginv, 14, 16)
 
     def solve(first, last):
         for j in range(first, last):

time: 102 us -> 98.7 us (0.968)
  Pallas kernels: 101 us -> 97.9 us
    pallas_call x1, Pallas kernels: 100 us -> 96.5 us  [per_device(): pl.pallas_call(kernel, name='semi_nmf', out_shape=(pltpu.VMEM((COMP, toke...]
where the time goes in v6:
time: 98.7 us; the launch traced here: 98.6 us
  Pallas kernels  97.9 us (99%)
    pallas_call x1, Pallas kernels, per_device(): pl.pallas_call(kernel, name='semi_nmf', out_shape=(pltpu.VMEM((COMP, toke...  96.5 us

profile of v6, /device:TPU:1, one launch (start us, length us, event | category | flops | bytes accessed | tf_op | source)
XLA Modules:
  0.0 98.6 jit_solution(17133089402638246188)
XLA Ops:
  0.6 96.5 %semi_nmf.1 = (f32[256,512]{1,0:T(8,128)S(1)}, f32[1792,256]{1,0:T(8,128)S(1)}) custom-call(bf16[512,1792]{1,0:T(8,128)(2,1)} %acts_in.1, f32[1792,256]{1,0:T(8,128)} %dic_in.1, f32[512,256]{1,0:T(8,128)} %codes_in.1), custom_call_target="tpu_custom_call" | custom-call | tf_op jit(solution)/shard_map/semi_nmf/pallas_call | solution.py:427
  97.1 1.4 %leave.1 = (f32[512,256]{1,0:T(8,128)}, f32[1792,256]{1,0:T(8,128)}) custom-call(f32[256,512]{1,0:T(8,128)S(1)} %get-tuple-element.4.out_t, f32[1792,256]{1,0:T(8,128)S(1)} %get-tuple-element.5.dict_in), custom_call_target="tpu_custom_call" | custom-call | tf_op jit(solution)/shard_map/leave/pallas_call | solution.py:452

commit v7 on v6

--- a/solution.py
+++ b/solution.py
@@ -87,8 +87,8 @@
 
 
 def part_list(halftiles):
-    b, c = halftiles - 2 * (halftiles * 2 // 7), halftiles * 2 // 7
-    return ((0, b, "xy"), (b, c, "xy"), (b + c, c, "yx"))
+    size = (halftiles - 1) * COMP // 2
+    return ((0, size, "xy"), (size, size, "xy"), (2 * size, COMP, "yx"))
 
 
 def kernel(
@@ -196,9 +196,10 @@
                     q = 8 + p - i * (pieces // 2)
                     held[4, i, p] = push(spot, spot, zs.at[phase, i, q], zr.at[phase, i, q], at(dz=2 * d + ZS))
                 held[3, i, p] = push(spot, spot, zs.at[phase, i, 10 + p], zr.at[phase, i, 10 + p], at(dz=d + ZS))
-        for key, c in held.items():
-            c.wait_send()
-            if key[0] != 2:
+
+    def arrive_z(held, half):
+        for (hops, i, p), c in held.items():
+            if hops != 2 and p // (pieces // 2) == half:
                 c.wait_recv()
 
     def send_gram(matrix, part, slots, sem):
@@ -256,29 +257,29 @@
     for c in held.values():
         c.wait_send()
     forward_z(mid, 1, passed)
-
-    low = mid[...].astype(jnp.bfloat16)
-    low_own = mid[own, :].astype(jnp.bfloat16)
-    gk[...] = lax.dot_general(low_own, low, NT, preferred_element_type=jnp.float32).reshape(gk.shape)
-    g_c = push(gk.at[1 - core], gk_c, cs.at[6], crs.at[6], at(dc=1))
+    arrive_z(passed, 0)
 
     halftiles = acts.shape[1] // 256
     parts = part_list(halftiles)
 
-    def cross(which, p):
-        first, count, _ = parts[p]
+    def low_half(half):
+        return jnp.concatenate([mid[chunk(j, 2 * half, 2), :] for j in range(ZS)], axis=0).astype(jnp.bfloat16)
+
+    def cross(which, p, codes_low):
+        first = 0 if p < 2 else halftiles - 1
+        count = halftiles - 1 if p < 2 else 1
         lanes = pl.ds(pl.multiple_of((which * halftiles + first) * 128, 128), count * 128)
-        block = jnp.dot(low, acts[:, lanes], preferred_element_type=jnp.float32)
+        block = jnp.dot(codes_low, acts[:, lanes], preferred_element_type=jnp.float32)
+        m = codes_low.shape[0]
         for j in range(count):
-            cr[which, pl.ds((first + j) * COMP, COMP), :] = block[:, j * 128 : j * 128 + 128]
+            cr[which, pl.ds(parts[p][0] + j * m, m), :] = block[:, j * 128 : j * 128 + 128]
 
     axes = {"x": (x, XS, xorder, xs, xr), "y": (y, YS, zorder, ys, yr)}
 
     def shares(p):
-        first, count, order = parts[p]
+        base, size, order = parts[p]
         one, two = axes[order[0]], axes[order[1]]
-        size = count * COMP
-        return first * COMP, size, one, two, size // one[1], size // one[1] // two[1]
+        return base, size, one, two, size // one[1], size // one[1] // two[1]
 
     def span_of(base, i, size):
         return pl.ds(pl.multiple_of(base + i * size, size), size)
@@ -329,15 +330,27 @@
         return [push(spot, spot, cs.at[3 + p], crs.at[3 + p], at(dc=1))]
 
     c = [None] * 3
-    for p in range(3):
-        cross(1 - core, p)
-        c[p] = send_core(p)
+    low0 = low_half(0)
+    cross(1 - core, 0, low0)
+    c[0] = send_core(0)
+    cross(core, 0, low0)
+    c[0] = send_first(0, c[0])
+    arrive_z(passed, 1)
+
+    low1 = low_half(1)
+    low = jnp.concatenate([low0, low1], axis=0)
+    low_own = mid[own, :].astype(jnp.bfloat16)
+    gk[...] = lax.dot_general(low_own, low, NT, preferred_element_type=jnp.float32).reshape(gk.shape)
+    g_c = push(gk.at[1 - core], gk_c, cs.at[6], crs.at[6], at(dc=1))
+    cross(1 - core, 1, low1)
+    c[1] = send_core(1)
+    cross(1 - core, 2, low)
+    c[2] = send_core(2)
     g_c.wait()
     gk_x[x] = gk[core] + gk_c[...]
     g_x = along("x", 6, lambda i: gk_x.at[x], lambda o: gk_x.at[x])
-    for p in range(3):
-        cross(core, p)
-    c[0] = send_first(0, c[0])
+    cross(core, 1, low1)
+    cross(core, 2, low)
     c[1] = send_first(1, c[1])
     finish(g_x)
     gk_y[y] = sum(gk_x[i] for i in range(XS))
@@ -346,42 +359,48 @@
     c[0] = send_second(0, c[0])
     c[1] = send_second(1, c[1])
     finish(g_y)
-    spot = gk_z.at[z, core]
+    spot = gk_z.at[core, z]
     spot[...] = sum(gk_y[i] for i in range(YS))
     g_z = [push(spot, spot, ds.at[2, o - 1], dr.at[2, o - 1], at(dz=o)) for o in zorder]
+    c[2] = send_second(2, c[2])
     c[0] = gather_second(0, c[0])
-    c[2] = send_second(2, c[2])
+    c[2] = gather_second(2, c[2])
     c[1] = gather_second(1, c[1])
+    c[0] = gather_first(0, c[0])
     finish(g_z)
-    spot = gk_z.at[:, core]
+    spot = gk_z.at[core]
     g_c = push(spot, spot, cs.at[7], crs.at[7], at(dc=1))
-    c[2] = gather_second(2, c[2])
+    c[2] = gather_first(2, c[2])
+    for copy in passed.values():
+        copy.wait_send()
     g_c.wait()
     ginv[...] = gk_z[...].reshape(COMP, COMP)
 
     invert_blocks(ginv, 0, 3)
-    c[0] = gather_first(0, c[0])
-    c[2] = gather_first(2, c[2])
-    invert_blocks(ginv, 3, 5)
     c[1] = gather_first(1, c[1])
-    invert_blocks(ginv, 5, 11)
+    invert_blocks(ginv, 3, 7)
     c[0] = gather_core(0, c[0])
-    invert_blocks(ginv, 11, 14)
+    c[2] = gather_core(2, c[2])
+    invert_blocks(ginv, 7, 13)
     c[1] = gather_core(1, c[1])
-    c[2] = gather_core(2, c[2])
-    invert_blocks(ginv, 14, 16)
-
-    def solve(first, last):
-        for j in range(first, last):
-            span = pl.ds(j * COMP, COMP)
-            block = jnp.concatenate([full[0, span, :], full[1, span, :]], axis=1)
-            solved = jnp.dot(ginv[...], block, precision=HIGHEST, preferred_element_type=jnp.float32)
+    invert_blocks(ginv, 13, 16)
+
+    half = COMP // 2
+    m = n // 2
+    inverse = jnp.concatenate([ginv[i * half + j * m : i * half + j * m + m, :] for j in range(ZS) for i in range(2)], axis=0)
+
+    def solve(tile_list):
+        for j, spots in tile_list:
+            pair = [jnp.concatenate([full[i, pl.ds(at0, half), :] for at0 in spots], axis=0) for i in range(2)]
+            solved = jnp.dot(inverse, jnp.concatenate(pair, axis=1), precision=HIGHEST, preferred_element_type=jnp.float32)
             for i in range(2):
                 dt[:, (i * halftiles + j) * 128 : (i * halftiles + j + 1) * 128] = solved[:, i * 128 : i * 128 + 128]
 
-    for p in (0, 2, 1):
-        finish(c[p])
-        solve(parts[p][0], parts[p][0] + parts[p][1])
+    finish(c[0])
+    finish(c[2])
+    solve([(halftiles - 1, (parts[2][0], parts[2][0] + half))])
+    finish(c[1])
+    solve([(j, (parts[0][0] + j * half, parts[1][0] + j * half)) for j in range(halftiles - 1)])
     sent_gram = send_gram(dt, gram2, gram2_in, 1)
     proj2[...] = lax.dot_general(dt[...].astype(jnp.bfloat16), acts[...], NT, preferred_element_type=jnp.float32)
     held = scatter_z(proj2, bufs2, 2)
@@ -396,6 +415,10 @@
     for c in held.values():
         c.wait_send()
     forward_z(out_t, 3, passed)
+    for half in range(2):
+        arrive_z(passed, half)
+    for c in passed.values():
+        c.wait_send()
 
 
 def leave(out_t, dict_in, codes_out, dict_out, held, sem):
@@ -419,7 +442,7 @@
     n = COMP // ZS
     half = hid * COMP // 2 // 128
     count = {"x": XS, "y": YS}
-    shapes = [(k * COMP, count[order[0]], count[order[1]]) for _, k, order in part_list(hid // 256)]
+    shapes = [(size, count[order[0]], count[order[1]]) for _, size, order in part_list(hid // 256)]
     sums = (v(2, n, tokens), v(2, n // 2, tokens), v(2, n, tokens), v(2, n, tokens), v(2, n, tokens))
     vmem = pl.BlockSpec(memory_space=pltpu.VMEM)
     anywhere = pl.BlockSpec(memory_space=pl.ANY)
@@ -434,7 +457,7 @@
             pltpu.VMEM((tokens, hid), jnp.bfloat16), v(hid, COMP), v(tokens, COMP), dma((3,)),
             v(COMP, hid), v(COMP, tokens), v(COMP, tokens), v(ZS, 8, 128),
             v(ZS - 1, 8, 128), v(2, XS, 8, 128), v(COMP, tokens),
-            v(2, n // 2, COMP), v(n // 2, COMP), v(XS, n // 2, COMP), v(YS, n // 2, COMP), v(ZS, 2, n // 2, COMP),
+            v(2, n // 2, COMP), v(n // 2, COMP), v(XS, n // 2, COMP), v(YS, n // 2, COMP), v(2, ZS, n // 2, COMP),
             v(COMP, COMP),
             v(2, half, 128), v(half, 128), v(2, half, 128),
             *[v(one - 1, size // one, 128) for size, one, two in shapes],

time: 98.7 us -> 100 us (1.013)
  Pallas kernels: 97.9 us -> 99.6 us
    pallas_call x1, Pallas kernels: 96.5 us -> 98.2 us  [per_device(): pl.pallas_call(kernel, name='semi_nmf', out_shape=(pltpu.VMEM((COMP, toke...]
where the time goes in v7:
time: 100 us
  Pallas kernels  99.6 us (100%)
    pallas_call x1, Pallas kernels, per_device(): pl.pallas_call(kernel, name='semi_nmf', out_shape=(pltpu.VMEM((COMP, toke...  98.2 us

profile of v7, /device:TPU:1, one launch (start us, length us, event | category | flops | bytes accessed | tf_op | source)
XLA Modules:
  0.0 100.3 jit_solution(13051167863708707739)
XLA Ops:
  0.6 98.2 %semi_nmf.1 = (f32[256,512]{1,0:T(8,128)S(1)}, f32[1792,256]{1,0:T(8,128)S(1)}) custom-call(bf16[512,1792]{1,0:T(8,128)(2,1)} %acts_in.1, f32[1792,256]{1,0:T(8,128)} %dic_in.1, f32[512,256]{1,0:T(8,128)} %codes_in.1), custom_call_target="tpu_custom_call" | custom-call | tf_op jit(solution)/shard_map/semi_nmf/pallas_call | solution.py:450
  98.8 1.4 %leave.1 = (f32[512,256]{1,0:T(8,128)}, f32[1792,256]{1,0:T(8,128)}) custom-call(f32[256,512]{1,0:T(8,128)S(1)} %get-tuple-element.4.out_t, f32[1792,256]{1,0:T(8,128)S(1)} %get-tuple-element.5.dict_in), custom_call_target="tpu_custom_call" | custom-call | tf_op jit(solution)/shard_map/leave/pallas_call | solution.py:475

commit v8 on v6

--- a/solution.py
+++ b/solution.py
@@ -87,8 +87,10 @@
 
 
 def part_list(halftiles):
-    b, c = halftiles - 2 * (halftiles * 2 // 7), halftiles * 2 // 7
-    return ((0, b, "xy"), (b, c, "xy"), (b + c, c, "yx"))
+    third = halftiles // 3
+    return (
+        (0, third, "xy"), (third, third, "xy"), (2 * third, third, "xy"), (3 * third, halftiles - 3 * third, "yx"),
+    )
 
 
 def kernel(
@@ -107,7 +109,7 @@
     zorder = (4, 3, 5, 2, 6, 1, 7)
     xorder = (2, 1, 3)
 
-    in1, sum1, in2, rest = rest[:3], rest[3:6], rest[6:9], rest[9:]
+    in1, sum1, in2, rest = rest[:4], rest[4:8], rest[8:12], rest[12:]
     (proj2, gram2, gram2_in, gram2_tiles), rest = rest[:4], rest[4:]
     bufs, bufs2, rest = rest[:5], rest[5:10], rest[10:]
     zs, zr, ds, dr, ys, yr, xs, xr, cs, crs = rest
@@ -246,9 +248,9 @@
     loads[2].wait()
     ct[...] = codes[...].T
     own = rows(z, n)
-    sent_gram = share_gram(sent_gram, gram, gram_in, gram_tiles, 7, 8)
+    sent_gram = share_gram(sent_gram, gram, gram_in, gram_tiles, 9, 10)
     relay_z(proj, bufs, 0, held)
-    prod = gram_products(whole_gram(sent_gram, gram_tiles, 7, 8), ct[...])
+    prod = gram_products(whole_gram(sent_gram, gram_tiles, 9, 10), ct[...])
     passed = {}
     for p in range(pieces):
         mid[chunk(z, p), :] = update(ct[chunk(z, p), :], summed_z(proj, bufs, held, p), prod, p)
@@ -260,7 +262,7 @@
     low = mid[...].astype(jnp.bfloat16)
     low_own = mid[own, :].astype(jnp.bfloat16)
     gk[...] = lax.dot_general(low_own, low, NT, preferred_element_type=jnp.float32).reshape(gk.shape)
-    g_c = push(gk.at[1 - core], gk_c, cs.at[6], crs.at[6], at(dc=1))
+    g_c = push(gk.at[1 - core], gk_c, cs.at[8], crs.at[8], at(dc=1))
 
     halftiles = acts.shape[1] // 256
     parts = part_list(halftiles)
@@ -326,48 +328,54 @@
         finish(copies)
         base, size, _, _, _, _ = shares(p)
         spot = full.at[core, pl.ds(base, size)]
-        return [push(spot, spot, cs.at[3 + p], crs.at[3 + p], at(dc=1))]
-
-    c = [None] * 3
-    for p in range(3):
+        return [push(spot, spot, cs.at[4 + p], crs.at[4 + p], at(dc=1))]
+
+    c = [None] * 4
+    for p in range(4):
         cross(1 - core, p)
         c[p] = send_core(p)
     g_c.wait()
     gk_x[x] = gk[core] + gk_c[...]
-    g_x = along("x", 6, lambda i: gk_x.at[x], lambda o: gk_x.at[x])
-    for p in range(3):
+    g_x = along("x", 8, lambda i: gk_x.at[x], lambda o: gk_x.at[x])
+    for p in range(4):
         cross(core, p)
     c[0] = send_first(0, c[0])
     c[1] = send_first(1, c[1])
+    c[2] = send_first(2, c[2])
     finish(g_x)
     gk_y[y] = sum(gk_x[i] for i in range(XS))
-    g_y = along("y", 6, lambda i: gk_y.at[y], lambda o: gk_y.at[y])
-    c[2] = send_first(2, c[2])
+    g_y = along("y", 8, lambda i: gk_y.at[y], lambda o: gk_y.at[y])
+    c[3] = send_first(3, c[3])
     c[0] = send_second(0, c[0])
     c[1] = send_second(1, c[1])
     finish(g_y)
     spot = gk_z.at[z, core]
     spot[...] = sum(gk_y[i] for i in range(YS))
     g_z = [push(spot, spot, ds.at[2, o - 1], dr.at[2, o - 1], at(dz=o)) for o in zorder]
+    c[2] = send_second(2, c[2])
     c[0] = gather_second(0, c[0])
-    c[2] = send_second(2, c[2])
+    c[3] = send_second(3, c[3])
     c[1] = gather_second(1, c[1])
+    c[2] = gather_second(2, c[2])
+    c[3] = gather_second(3, c[3])
     finish(g_z)
     spot = gk_z.at[:, core]
-    g_c = push(spot, spot, cs.at[7], crs.at[7], at(dc=1))
-    c[2] = gather_second(2, c[2])
+    g_c = push(spot, spot, cs.at[9], crs.at[9], at(dc=1))
+    c[0] = gather_first(0, c[0])
     g_c.wait()
     ginv[...] = gk_z[...].reshape(COMP, COMP)
 
-    invert_blocks(ginv, 0, 3)
-    c[0] = gather_first(0, c[0])
+    invert_blocks(ginv, 0, 2)
+    c[1] = gather_first(1, c[1])
+    c[3] = gather_first(3, c[3])
+    invert_blocks(ginv, 2, 5)
     c[2] = gather_first(2, c[2])
-    invert_blocks(ginv, 3, 5)
-    c[1] = gather_first(1, c[1])
-    invert_blocks(ginv, 5, 11)
+    invert_blocks(ginv, 5, 7)
     c[0] = gather_core(0, c[0])
+    invert_blocks(ginv, 7, 11)
+    c[1] = gather_core(1, c[1])
     invert_blocks(ginv, 11, 14)
-    c[1] = gather_core(1, c[1])
+    c[3] = gather_core(3, c[3])
     c[2] = gather_core(2, c[2])
     invert_blocks(ginv, 14, 16)
 
@@ -379,16 +387,16 @@
             for i in range(2):
                 dt[:, (i * halftiles + j) * 128 : (i * halftiles + j + 1) * 128] = solved[:, i * 128 : i * 128 + 128]
 
-    for p in (0, 2, 1):
+    for p in (0, 1, 3, 2):
         finish(c[p])
         solve(parts[p][0], parts[p][0] + parts[p][1])
     sent_gram = send_gram(dt, gram2, gram2_in, 1)
     proj2[...] = lax.dot_general(dt[...].astype(jnp.bfloat16), acts[...], NT, preferred_element_type=jnp.float32)
     held = scatter_z(proj2, bufs2, 2)
     dict_out[...] = dt[...].T
-    sent_gram = share_gram(sent_gram, gram2, gram2_in, gram2_tiles, 8, 9)
+    sent_gram = share_gram(sent_gram, gram2, gram2_in, gram2_tiles, 10, 11)
     relay_z(proj2, bufs2, 2, held)
-    prod = gram_products(whole_gram(sent_gram, gram2_tiles, 8, 9), mid[...])
+    prod = gram_products(whole_gram(sent_gram, gram2_tiles, 10, 11), mid[...])
     passed = {}
     for p in range(pieces):
         out_t[chunk(z, p), :] = update(mid[chunk(z, p), :], summed_z(proj2, bufs2, held, p), prod, p)
@@ -442,8 +450,8 @@
             *[v(two - 1, size // one // two, 128) for size, one, two in shapes],
             v(COMP, tokens), v(ZS, 8, 128), v(ZS - 1, 8, 128), v(2, XS, 8, 128),
             *sums, *sums,
-            dma((4, 2, 14)), dma((4, 2, 14)), dma((3, ZS - 1)), dma((3, ZS - 1)), dma((7, YS - 1)), dma((7, YS - 1)),
-            dma((9, XS - 1)), dma((9, XS - 1)), dma((10,)), dma((10,)),
+            dma((4, 2, 14)), dma((4, 2, 14)), dma((3, ZS - 1)), dma((3, ZS - 1)), dma((9, YS - 1)), dma((9, YS - 1)),
+            dma((11, XS - 1)), dma((11, XS - 1)), dma((12,)), dma((12,)),
         ],
         compiler_params=pltpu.CompilerParams(
             collective_id=0, has_side_effects=True, vmem_limit_bytes=56 * 1024 * 1024

time: 98.7 us -> 97.1 us (0.984)
  Pallas kernels: 97.9 us -> 96.4 us
    pallas_call x1, Pallas kernels: 96.5 us -> 94.9 us  [per_device(): pl.pallas_call(kernel, name='semi_nmf', out_shape=(pltpu.VMEM((COMP, toke...]
where the time goes in v8:
time: 97.1 us; the launch traced here: 97 us
  Pallas kernels  96.4 us (99%)
    pallas_call x1, Pallas kernels, per_device(): pl.pallas_call(kernel, name='semi_nmf', out_shape=(pltpu.VMEM((COMP, toke...  94.9 us

profile of v8, /device:TPU:1, one launch (start us, length us, event | category | flops | bytes accessed | tf_op | source)
XLA Modules:
  0.0 97.0 jit_solution(591377759048028352)
XLA Ops:
  0.6 94.9 %semi_nmf.1 = (f32[256,512]{1,0:T(8,128)S(1)}, f32[1792,256]{1,0:T(8,128)S(1)}) custom-call(bf16[512,1792]{1,0:T(8,128)(2,1)} %acts_in.1, f32[1792,256]{1,0:T(8,128)} %dic_in.1, f32[512,256]{1,0:T(8,128)} %codes_in.1), custom_call_target="tpu_custom_call" | custom-call | tf_op jit(solution)/shard_map/semi_nmf/pallas_call | solution.py:435
  95.6 1.4 %leave.1 = (f32[512,256]{1,0:T(8,128)}, f32[1792,256]{1,0:T(8,128)}) custom-call(f32[256,512]{1,0:T(8,128)S(1)} %get-tuple-element.4.out_t, f32[1792,256]{1,0:T(8,128)S(1)} %get-tuple-element.5.dict_in), custom_call_target="tpu_custom_call" | custom-call | tf_op jit(solution)/shard_map/leave/pallas_call | solution.py:460

commit v9 on v8

--- a/solution.py
+++ b/solution.py
@@ -203,30 +203,30 @@
             if key[0] != 2:
                 c.wait_recv()
 
-    def send_gram(matrix, part, slots, sem):
+    def make_gram(matrix, part):
         picked = [matrix[pl.ds(pl.multiple_of(j * n + x * 8, 8), 8), :] for j in range(ZS)]
         both = split2(jnp.concatenate(picked, axis=0))
-        prod = lax.dot_general(both, split2(matrix[rows(core, 128), :]), NT, preferred_element_type=jnp.float32)
+        prod = lax.dot_general(both, split2(matrix[...]), NT, preferred_element_type=jnp.float32)
         m = 8 * ZS
-        tile = prod[:m, :128] + (prod[:m, 128:] + prod[m:, :128] + prod[m:, 128:])
+        tile = prod[:m, :COMP] + (prod[:m, COMP:] + prod[m:, :COMP] + prod[m:, COMP:])
         part[...] = tile.reshape(part.shape)
+
+    def send_gram(part, slots, sem):
         out = []
         for o in zorder:
             dev = at(dz=o)
             out.append(push(part.at[dev[1]], slots.at[o - 1], ds.at[sem, o - 1], dr.at[sem, o - 1], dev))
         return out
 
-    def share_gram(sent, part, slots, tiles, step, _):
+    def share_gram(sent, part, slots, tiles, step):
         finish(sent)
-        spot = tiles.at[core, x]
+        spot = tiles.at[x]
         spot[...] = part[z] + sum(slots[i] for i in range(ZS - 1))
         return [push(spot, spot, xs.at[step, o - 1], xr.at[step, o - 1], at(dx=o)) for o in xorder]
 
-    def whole_gram(sent, tiles, _, step):
+    def whole_gram(sent, tiles):
         finish(sent)
-        spot = tiles.at[core]
-        push(spot, spot, cs.at[step], crs.at[step], at(dc=1)).wait()
-        return jnp.concatenate([tiles[i].reshape(n, 128) for i in range(2)], axis=1)
+        return tiles[...].reshape(n, COMP)
 
     def finish(copies):
         for c in copies:
@@ -240,17 +240,18 @@
         c.start()
     loads[0].wait()
     dt[...] = dic[...].T
+    make_gram(dt, gram)
     loads[1].wait()
     proj[...] = lax.dot_general(dt[...].astype(jnp.bfloat16), acts[...], NT, preferred_element_type=jnp.float32)
     pl.semaphore_wait(barrier, len(partners))
-    sent_gram = send_gram(dt, gram, gram_in, 0)
+    sent_gram = send_gram(gram, gram_in, 0)
     held = scatter_z(proj, bufs, 0)
     loads[2].wait()
     ct[...] = codes[...].T
     own = rows(z, n)
-    sent_gram = share_gram(sent_gram, gram, gram_in, gram_tiles, 9, 10)
+    sent_gram = share_gram(sent_gram, gram, gram_in, gram_tiles, 9)
     relay_z(proj, bufs, 0, held)
-    prod = gram_products(whole_gram(sent_gram, gram_tiles, 9, 10), ct[...])
+    prod = gram_products(whole_gram(sent_gram, gram_tiles), ct[...])
     passed = {}
     for p in range(pieces):
         mid[chunk(z, p), :] = update(ct[chunk(z, p), :], summed_z(proj, bufs, held, p), prod, p)
@@ -390,13 +391,14 @@
     for p in (0, 1, 3, 2):
         finish(c[p])
         solve(parts[p][0], parts[p][0] + parts[p][1])
-    sent_gram = send_gram(dt, gram2, gram2_in, 1)
+    make_gram(dt, gram2)
+    sent_gram = send_gram(gram2, gram2_in, 1)
     proj2[...] = lax.dot_general(dt[...].astype(jnp.bfloat16), acts[...], NT, preferred_element_type=jnp.float32)
     held = scatter_z(proj2, bufs2, 2)
     dict_out[...] = dt[...].T
-    sent_gram = share_gram(sent_gram, gram2, gram2_in, gram2_tiles, 10, 11)
+    sent_gram = share_gram(sent_gram, gram2, gram2_in, gram2_tiles, 10)
     relay_z(proj2, bufs2, 2, held)
-    prod = gram_products(whole_gram(sent_gram, gram2_tiles, 10, 11), mid[...])
+    prod = gram_products(whole_gram(sent_gram, gram2_tiles), mid[...])
     passed = {}
     for p in range(pieces):
         out_t[chunk(z, p), :] = update(mid[chunk(z, p), :], summed_z(proj2, bufs2, held, p), prod, p)
@@ -440,15 +442,15 @@
         out_specs=(vmem, vmem),
         scratch_shapes=[
             pltpu.VMEM((tokens, hid), jnp.bfloat16), v(hid, COMP), v(tokens, COMP), dma((3,)),
-            v(COMP, hid), v(COMP, tokens), v(COMP, tokens), v(ZS, 8, 128),
-            v(ZS - 1, 8, 128), v(2, XS, 8, 128), v(COMP, tokens),
+            v(COMP, hid), v(COMP, tokens), v(COMP, tokens), v(ZS, 8, COMP),
+            v(ZS - 1, 8, COMP), v(XS, 8, COMP), v(COMP, tokens),
             v(2, n // 2, COMP), v(n // 2, COMP), v(XS, n // 2, COMP), v(YS, n // 2, COMP), v(ZS, 2, n // 2, COMP),
             v(COMP, COMP),
             v(2, half, 128), v(half, 128), v(2, half, 128),
             *[v(one - 1, size // one, 128) for size, one, two in shapes],
             *[v(size // one, 128) for size, one, two in shapes],
             *[v(two - 1, size // one // two, 128) for size, one, two in shapes],
-            v(COMP, tokens), v(ZS, 8, 128), v(ZS - 1, 8, 128), v(2, XS, 8, 128),
+            v(COMP, tokens), v(ZS, 8, COMP), v(ZS - 1, 8, COMP), v(XS, 8, COMP),
             *sums, *sums,
             dma((4, 2, 14)), dma((4, 2, 14)), dma((3, ZS - 1)), dma((3, ZS - 1)), dma((9, YS - 1)), dma((9, YS - 1)),
             dma((11, XS - 1)), dma((11, XS - 1)), dma((12,)), dma((12,)),

time: 97.1 us -> 96.1 us (0.990); the launches traced: 97 us -> 94.3 us
  Pallas kernels: 96.4 us -> 93.6 us
    pallas_call x1, Pallas kernels: 94.9 us -> 92.2 us  [per_device(): pl.pallas_call(kernel, name='semi_nmf', out_shape=(pltpu.VMEM((COMP, toke...]
where the time goes in v9:
time: 96.1 us; the launch traced here: 94.3 us
  Pallas kernels  93.6 us (97%)
    pallas_call x1, Pallas kernels, per_device(): pl.pallas_call(kernel, name='semi_nmf', out_shape=(pltpu.VMEM((COMP, toke...  92.2 us

profile of v9, /device:TPU:1, one launch (start us, length us, event | category | flops | bytes accessed | tf_op | source)
XLA Modules:
  0.0 94.3 jit_solution(2276758858421548632)
XLA Ops:
  0.6 92.2 %semi_nmf.1 = (f32[256,512]{1,0:T(8,128)S(1)}, f32[1792,256]{1,0:T(8,128)S(1)}) custom-call(bf16[512,1792]{1,0:T(8,128)(2,1)} %acts_in.1, f32[1792,256]{1,0:T(8,128)} %dic_in.1, f32[512,256]{1,0:T(8,128)} %codes_in.1), custom_call_target="tpu_custom_call" | custom-call | tf_op jit(solution)/shard_map/semi_nmf/pallas_call | solution.py:437
  92.8 1.4 %leave.1 = (f32[512,256]{1,0:T(8,128)}, f32[1792,256]{1,0:T(8,128)}) custom-call(f32[256,512]{1,0:T(8,128)S(1)} %get-tuple-element.4.out_t, f32[1792,256]{1,0:T(8,128)S(1)} %get-tuple-element.5.dict_in), custom_call_target="tpu_custom_call" | custom-call | tf_op jit(solution)/shard_map/leave/pallas_call | solution.py:462

commit v10 on v9

--- a/solution.py
+++ b/solution.py
@@ -75,8 +75,12 @@
 
 
 def gram_products(gram, codes):
-    both = jnp.concatenate([jnp.maximum(-gram, 0.0), jnp.maximum(gram, 0.0)], axis=0)
-    return jnp.dot(both, codes, precision=HIGHEST, preferred_element_type=jnp.float32)
+    both = split2(jnp.concatenate([jnp.maximum(-gram, 0.0), jnp.maximum(gram, 0.0)], axis=0))
+    hi = codes.astype(jnp.bfloat16)
+    low = (codes - hi.astype(jnp.float32)).astype(jnp.bfloat16)
+    prod = jnp.dot(both, low, preferred_element_type=jnp.float32) + jnp.dot(both, hi, preferred_element_type=jnp.float32)
+    m = 2 * gram.shape[0]
+    return prod[:m] + prod[m:]
 
 
 def update(part, proj, prod, p):

time: 96.1 us -> 96.4 us (level)
  no operation moved by 1% of the time
where the time goes in v10:
time: 96.4 us; the launch traced here: 94.9 us
  Pallas kernels  94.2 us (98%)
    pallas_call x1, Pallas kernels, per_device(): pl.pallas_call(kernel, name='semi_nmf', out_shape=(pltpu.VMEM((COMP, toke...  92.8 us

profile of v10, /device:TPU:1, one launch (start us, length us, event | category | flops | bytes accessed | tf_op | source)
XLA Modules:
  0.0 94.9 jit_solution(8557897545710038065)
XLA Ops:
  0.6 92.8 %semi_nmf.1 = (f32[256,512]{1,0:T(8,128)S(1)}, f32[1792,256]{1,0:T(8,128)S(1)}) custom-call(bf16[512,1792]{1,0:T(8,128)(2,1)} %acts_in.1, f32[1792,256]{1,0:T(8,128)} %dic_in.1, f32[512,256]{1,0:T(8,128)} %codes_in.1), custom_call_target="tpu_custom_call" | custom-call | tf_op jit(solution)/shard_map/semi_nmf/pallas_call | solution.py:441
  93.4 1.4 %leave.1 = (f32[512,256]{1,0:T(8,128)}, f32[1792,256]{1,0:T(8,128)}) custom-call(f32[256,512]{1,0:T(8,128)S(1)} %get-tuple-element.4.out_t, f32[1792,256]{1,0:T(8,128)S(1)} %get-tuple-element.5.dict_in), custom_call_target="tpu_custom_call" | custom-call | tf_op jit(solution)/shard_map/leave/pallas_call | solution.py:466
